TPU v7x, 32 devices: a whole 2x2x4 slice. The times are simulated.
32 devices in a mesh: dp: 16 (over z, y, x), ctx: 2 (over core).
Axes of the slice: x: 2, y: 2, z: 4, core: 2. Of those that a mesh axis runs over, the one named last changes fastest.
Arguments:
- tokens_in: bfloat16 [16, 1024, 768], P('dp', 'ctx'), may hold values from -6 to 6
- cond_vec: bfloat16 [16, 128], P('dp'), may hold values from -6 to 6
- positions: int32 [16, 1024], P('dp', 'ctx'), may hold values from 0 to 3069, as said below
- absorbed: int32 [16, 1024], P('dp', 'ctx'), may hold values 0 or 1
- cotangent: bfloat16 [16, 1024, 768], P('dp', 'ctx'), may hold values from -6 to 6
- norm1_gain: bfloat16 [768], replicated, may hold values from 0.5 to 1.5
- qkv_weight: bfloat16 [768, 2304], replicated, may hold values from -0.21875 to 0.21875
- out_weight: bfloat16 [768, 768], replicated, may hold values from -0.875 to 0.875
- norm2_gain: bfloat16 [768], replicated, may hold values from 0.5 to 1.5
- fc1_weight: bfloat16 [768, 3072], replicated, may hold values from -0.21875 to 0.21875
- fc1_bias: bfloat16 [3072], replicated, may hold values from -1.75 to 1.75
- fc2_weight: bfloat16 [3072, 768], replicated, may hold values from -0.109375 to 0.109375
- fc2_bias: bfloat16 [768], replicated, may hold values from -1.75 to 1.75
- ada_weight: bfloat16 [128, 4608], replicated, may hold values from -0.25 to 0.25
- ada_bias: bfloat16 [4608], replicated, may hold values from -1.75 to 1.75
Outputs:
- mixed: bfloat16 [16, 1024, 768], P('dp', 'ctx')
- input_grad: bfloat16 [16, 1024, 768], P('dp', 'ctx')
- cond_grad: float32 [16, 128], P('dp')
- norm1_gain_grad: float32 [768], P('dp')
- qkv_grad: float32 [768, 2304], P('dp')
- out_grad: float32 [768, 768], P('dp')
- norm2_gain_grad: float32 [768], P('dp')
- fc1_grad: float32 [768, 3072], P('dp')
- fc1_bias_grad: float32 [3072], P('dp')
- fc2_grad: float32 [3072, 768], P('dp')
- fc2_bias_grad: float32 [768], P('dp')
- ada_grad: float32 [128, 4608], P(None, 'dp')
- ada_bias_grad: float32 [4608], P('dp')
Inputs may be any that keep to these rules, and one draw needn't show every extreme that they name: In each sequence the positions start at 0 and rise by 1 to 3 from one token to the next.
All inputs are finite; a program needn't handle non-finite values. No bound on the sum of `absorbed` on one device may be relied on, other than what follows from the above.
Results may differ from a plain program's by a relative error of at most 0.019.
Values may be sent and summed in bfloat16 or wider, within the bound.
No kernel may reach another device: no remote copies, remote signals or barrier semaphores. Data moves between devices by JAX's collectives and lax.ppermute only.
A program may use at most 192 MiB of HBM per device.

v0:
```python
import jax
import jax.numpy as jnp
from jax import lax
from jax.sharding import PartitionSpec as P

HEADS = 12
HEAD_DIM = 64


EPS = 1e-05
SCORE_SCALE = 0.125
NEG_START = -1e30


def layer_norm(stream):
    row_mean = jnp.mean(stream, axis=-1, keepdims=True)
    centred = stream - row_mean
    variance = jnp.mean(centred * centred, axis=-1, keepdims=True)
    return centred * lax.rsqrt(variance + EPS)


def pre_norm(stream, norm_gain, shift_vec, scale_vec):
    return layer_norm(stream) * norm_gain * (1.0 + scale_vec[:, None, :]) + shift_vec[:, None, :]


def gelu_tanh(stream):
    return jax.nn.gelu(stream, approximate=True)


def block_rows(row_count):
    size_now = row_count
    while size_now > 512 and size_now % 2 == 0:
        size_now = size_now // 2
    return size_now


def rotary_tables(positions):
    inv_freq = 10000.0 ** (-jnp.arange(0, HEAD_DIM, 2).astype(jnp.float32) / HEAD_DIM)
    angles = positions.astype(jnp.float32)[..., None] * inv_freq
    cos_table = jnp.concatenate([jnp.cos(angles), jnp.cos(angles)], axis=-1)[..., None, :]
    sin_table = jnp.concatenate([jnp.sin(angles), jnp.sin(angles)], axis=-1)[..., None, :]
    return (cos_table, sin_table)


def rotate_pos(stream, cos_table, sin_table):
    half_dim = stream.shape[-1] // 2
    turned = jnp.concatenate([-stream[..., half_dim:], stream[..., :half_dim]], axis=-1)
    return stream * cos_table + turned * sin_table


def over_blocks(step_fn, fold_state, pieces):
    row_count = pieces[0].shape[1]
    size_now = block_rows(row_count)

    def one_turn(turn_idx, inner_state):
        part_list = tuple(
            (
                lax.dynamic_slice_in_dim(member, turn_idx * size_now, size_now, 1)
                for member in pieces
            )
        )
        return step_fn(inner_state, part_list, turn_idx * size_now)

    return lax.fori_loop(0, row_count // size_now, one_turn, fold_state)


def score_grads(query_blk, key_blk, value_blk, grad_blk, top_blk, total_blk, delta_blk):
    scores = (
        jnp.einsum("sqhd,skhd->sqhk", query_blk, key_blk, preferred_element_type=jnp.float32)
        * SCORE_SCALE
    )
    probability = jnp.exp(scores - top_blk[..., None]) / total_blk[..., None]
    grad_prob = jnp.einsum(
        "sqhd,skhd->sqhk", grad_blk, value_blk, preferred_element_type=jnp.float32
    )
    grad_scores = (probability * (grad_prob - delta_blk[..., None])).astype(jnp.bfloat16)
    return (probability, grad_scores)


def local(
    tokens_in,
    cond_vec,
    positions,
    absorbed,
    cotangent,
    norm1_gain,
    qkv_weight,
    out_weight,
    norm2_gain,
    fc1_weight,
    fc1_bias,
    fc2_weight,
    fc2_bias,
    ada_weight,
    ada_bias,
):
    seqs_here, span_len, model_width = tokens_in.shape
    head_shape = (seqs_here, span_len, HEADS, HEAD_DIM)
    stream = tokens_in.astype(jnp.float32)
    modulation = jnp.dot(
        cond_vec, ada_weight, preferred_element_type=jnp.float32
    ) + ada_bias.astype(jnp.float32)
    shift_one, scale_one, gate_one, shift_two, scale_two, gate_two = jnp.split(
        modulation, 6, axis=-1
    )
    gain_one = norm1_gain.astype(jnp.float32)
    gain_two = norm2_gain.astype(jnp.float32)
    normed_f, pull_one = jax.vjp(pre_norm, stream, gain_one, shift_one, scale_one)
    normed_one = normed_f.astype(jnp.bfloat16)
    projected = jnp.dot(normed_one, qkv_weight, preferred_element_type=jnp.float32)
    cos_table, sin_table = rotary_tables(positions)
    turned_pair, pull_rot = jax.vjp(
        lambda query_pre, key_pre: (
            rotate_pos(query_pre, cos_table, sin_table),
            rotate_pos(key_pre, cos_table, sin_table),
        ),
        projected[..., :model_width].reshape(head_shape),
        projected[..., model_width : 2 * model_width].reshape(head_shape),
    )
    queries = turned_pair[0].astype(jnp.bfloat16)
    key_loc = turned_pair[1].astype(jnp.bfloat16).reshape(seqs_here, span_len, model_width)
    value_loc = projected[..., 2 * model_width :].astype(jnp.bfloat16)

    def forward_step(fold_state, part_list, offset):
        run_max, run_sum, run_acc = fold_state
        key_blk = part_list[0].reshape(seqs_here, -1, HEADS, HEAD_DIM)
        value_blk = part_list[1].reshape(seqs_here, -1, HEADS, HEAD_DIM)
        scores = (
            jnp.einsum("sqhd,skhd->sqhk", queries, key_blk, preferred_element_type=jnp.float32)
            * SCORE_SCALE
        )
        new_max = jnp.maximum(run_max, jnp.max(scores, axis=-1))
        raised = jnp.exp(scores - new_max[..., None])
        shrink = jnp.exp(run_max - new_max)
        run_sum = run_sum * shrink + jnp.sum(raised, axis=-1)
        run_acc = run_acc * shrink[..., None] + jnp.einsum(
            "sqhk,skhd->sqhd",
            raised.astype(jnp.bfloat16),
            value_blk,
            preferred_element_type=jnp.float32,
        )
        return (new_max, run_sum, run_acc)

    empty_state = (
        jnp.full((seqs_here, span_len, HEADS), NEG_START, jnp.float32),
        jnp.zeros((seqs_here, span_len, HEADS), jnp.float32),
        jnp.zeros(head_shape, jnp.float32),
    )
    final_max, final_sum, final_acc = over_blocks(
        forward_step,
        empty_state,
        (
            lax.all_gather(key_loc, "ctx", axis=1, tiled=True),
            lax.all_gather(value_loc, "ctx", axis=1, tiled=True),
        ),
    )
    attn_out = final_acc / final_sum[..., None]
    attended = attn_out.reshape(seqs_here, span_len, model_width).astype(jnp.bfloat16)
    branch_att = jnp.dot(attended, out_weight, preferred_element_type=jnp.float32)
    middle = stream + gate_one[:, None, :] * branch_att
    normed_f2, pull_two = jax.vjp(pre_norm, middle, gain_two, shift_two, scale_two)
    normed_two = normed_f2.astype(jnp.bfloat16)
    hidden_pre = jnp.dot(
        normed_two, fc1_weight, preferred_element_type=jnp.float32
    ) + fc1_bias.astype(jnp.float32)
    hidden_f, pull_gelu = jax.vjp(gelu_tanh, hidden_pre)
    hidden = hidden_f.astype(jnp.bfloat16)
    branch_mlp = jnp.dot(hidden, fc2_weight, preferred_element_type=jnp.float32) + fc2_bias.astype(
        jnp.float32
    )
    mixed = (middle + gate_two[:, None, :] * branch_mlp).astype(jnp.bfloat16)
    weighted = cotangent.astype(jnp.float32) * absorbed.astype(jnp.float32)[..., None]
    grad_gate_two = jnp.sum(weighted * branch_mlp, axis=1)
    grad_mlp = (weighted * gate_two[:, None, :]).astype(jnp.bfloat16)
    grad_fc2b = jnp.sum(grad_mlp.astype(jnp.float32), axis=(0, 1))
    grad_fc2 = jnp.einsum("scf,scd->fd", hidden, grad_mlp, preferred_element_type=jnp.float32)
    grad_hidden = jnp.einsum(
        "scd,fd->scf", grad_mlp, fc2_weight, preferred_element_type=jnp.float32
    )
    grad_pre = pull_gelu(grad_hidden)[0].astype(jnp.bfloat16)
    grad_fc1b = jnp.sum(grad_pre.astype(jnp.float32), axis=(0, 1))
    grad_fc1 = jnp.einsum("scd,scf->df", normed_two, grad_pre, preferred_element_type=jnp.float32)
    grad_normed_two = jnp.einsum(
        "scf,df->scd", grad_pre, fc1_weight, preferred_element_type=jnp.float32
    )
    grad_mid_part, grad_gain_two, grad_shift_two, grad_scale_two = pull_two(grad_normed_two)
    grad_middle = weighted + grad_mid_part
    grad_gate_one = jnp.sum(grad_middle * branch_att, axis=1)
    grad_att = (grad_middle * gate_one[:, None, :]).astype(jnp.bfloat16)
    grad_out = jnp.einsum("scd,sce->de", attended, grad_att, preferred_element_type=jnp.float32)
    grad_attended = (
        jnp.einsum("sce,de->scd", grad_att, out_weight, preferred_element_type=jnp.float32)
        .astype(jnp.bfloat16)
        .reshape(head_shape)
    )
    row_delta = jnp.sum(grad_attended.astype(jnp.float32) * attn_out, axis=-1)

    def query_only_step(fold_state, part_list, offset):
        piece_len = part_list[0].shape[1]
        key_blk = part_list[0].reshape(seqs_here, piece_len, HEADS, HEAD_DIM)
        value_blk = part_list[1].reshape(seqs_here, piece_len, HEADS, HEAD_DIM)
        probability, grad_scores = score_grads(
            queries, key_blk, value_blk, grad_attended, final_max, final_sum, row_delta
        )
        return (
            fold_state
            + jnp.einsum(
                "sqhk,skhd->sqhd", grad_scores, key_blk, preferred_element_type=jnp.float32
            )
            * SCORE_SCALE
        )

    start_state = jnp.zeros(head_shape, jnp.float32)
    back_state = over_blocks(
        query_only_step,
        start_state,
        (
            lax.all_gather(key_loc, "ctx", axis=1, tiled=True),
            lax.all_gather(value_loc, "ctx", axis=1, tiled=True),
        ),
    )
    key_heads = key_loc.reshape(head_shape)
    value_heads = value_loc.reshape(head_shape)

    def local_key_step(fold_state, part_list, offset):
        grad_key_loc, grad_value_loc = fold_state
        query_blk = part_list[0].astype(jnp.bfloat16)
        grad_blk = part_list[1].astype(jnp.bfloat16)
        probability, grad_scores = score_grads(
            query_blk, key_heads, value_heads, grad_blk, part_list[2], part_list[3], part_list[4]
        )
        grad_value_loc = grad_value_loc + jnp.einsum(
            "sqhk,sqhd->skhd",
            probability.astype(jnp.bfloat16),
            grad_blk,
            preferred_element_type=jnp.float32,
        )
        grad_key_loc = (
            grad_key_loc
            + jnp.einsum(
                "sqhk,sqhd->skhd", grad_scores, query_blk, preferred_element_type=jnp.float32
            )
            * SCORE_SCALE
        )
        return (grad_key_loc, grad_value_loc)

    key_start = (jnp.zeros(head_shape, jnp.float32), jnp.zeros(head_shape, jnp.float32))
    grad_key_h, grad_value_h = over_blocks(
        local_key_step,
        key_start,
        (
            lax.all_gather(queries.astype(jnp.float32), "ctx", axis=1, tiled=True),
            lax.all_gather(grad_attended.astype(jnp.float32), "ctx", axis=1, tiled=True),
            lax.all_gather(final_max, "ctx", axis=1, tiled=True),
            lax.all_gather(final_sum, "ctx", axis=1, tiled=True),
            lax.all_gather(row_delta, "ctx", axis=1, tiled=True),
        ),
    )
    grad_key_loc = grad_key_h.reshape(seqs_here, span_len, model_width)
    grad_value_loc = grad_value_h.reshape(seqs_here, span_len, model_width)
    grad_query_pre, grad_key_pre = pull_rot((back_state, grad_key_loc.reshape(head_shape)))
    grad_proj = jnp.concatenate(
        [
            grad_query_pre.reshape(seqs_here, span_len, model_width),
            grad_key_pre.reshape(seqs_here, span_len, model_width),
            grad_value_loc,
        ],
        axis=-1,
    ).astype(jnp.bfloat16)
    grad_qkv = jnp.einsum("scd,sce->de", normed_one, grad_proj, preferred_element_type=jnp.float32)
    grad_normed_one = jnp.einsum(
        "sce,de->scd", grad_proj, qkv_weight, preferred_element_type=jnp.float32
    )
    grad_in_part, grad_gain_one, grad_shift_one, grad_scale_one = pull_one(grad_normed_one)
    input_grad = (grad_middle + grad_in_part).astype(jnp.bfloat16)
    partial_mod = jnp.concatenate(
        [
            grad_shift_one,
            grad_scale_one,
            grad_gate_one,
            grad_shift_two,
            grad_scale_two,
            grad_gate_two,
        ],
        axis=-1,
    )
    grad_mod = lax.psum(partial_mod, "ctx")
    cond_grad = jnp.einsum(
        "se,ce->sc",
        grad_mod,
        ada_weight.astype(jnp.float32),
        precision=lax.Precision.HIGHEST,
        preferred_element_type=jnp.float32,
    )
    first_cycle = (lax.axis_index("ctx") == 0).astype(jnp.float32)
    grad_ada = (
        jnp.einsum(
            "sc,se->ce",
            cond_vec.astype(jnp.float32),
            grad_mod,
            precision=lax.Precision.HIGHEST,
            preferred_element_type=jnp.float32,
        )
        * first_cycle
    )
    grad_adab = jnp.sum(grad_mod, axis=0) * first_cycle
    (
        part_g1,
        part_qkv,
        part_out,
        part_g2,
        part_fc1,
        part_fc1b,
        part_fc2,
        part_fc2b,
        part_ada,
        part_adab,
    ) = (
        lax.psum_scatter(grad_gain_one, "dp", scatter_dimension=0, tiled=True),
        lax.psum_scatter(grad_qkv, "dp", scatter_dimension=0, tiled=True),
        lax.psum_scatter(grad_out, "dp", scatter_dimension=0, tiled=True),
        lax.psum_scatter(grad_gain_two, "dp", scatter_dimension=0, tiled=True),
        lax.psum_scatter(grad_fc1, "dp", scatter_dimension=0, tiled=True),
        lax.psum_scatter(grad_fc1b, "dp", scatter_dimension=0, tiled=True),
        lax.psum_scatter(grad_fc2, "dp", scatter_dimension=0, tiled=True),
        lax.psum_scatter(grad_fc2b, "dp", scatter_dimension=0, tiled=True),
        lax.psum_scatter(grad_ada, "dp", scatter_dimension=1, tiled=True),
        lax.psum_scatter(grad_adab, "dp", scatter_dimension=0, tiled=True),
    )
    summed = lax.psum(
        (
            part_g1,
            part_qkv,
            part_out,
            part_g2,
            part_fc1,
            part_fc1b,
            part_fc2,
            part_fc2b,
            part_ada,
            part_adab,
        ),
        "ctx",
    )
    return (mixed, input_grad, cond_grad) + tuple(summed)


def solution(mesh):
    in_specs = (
        P("dp", "ctx", None),
        P("dp", None),
        P("dp", "ctx"),
        P("dp", "ctx"),
        P("dp", "ctx", None),
        P(),
        P(),
        P(),
        P(),
        P(),
        P(),
        P(),
        P(),
        P(),
        P(),
    )
    out_specs = (
        P("dp", "ctx", None),
        P("dp", "ctx", None),
        P("dp", None),
        P("dp"),
        P("dp", None),
        P("dp", None),
        P("dp"),
        P("dp", None),
        P("dp"),
        P("dp", None),
        P("dp"),
        P(None, "dp"),
        P("dp"),
    )
    return jax.shard_map(local, mesh=mesh, in_specs=in_specs, out_specs=out_specs, check_vma=False)
```

profile of v0, /device:TPU:0, one launch (start us, length us, event | category | flops | bytes accessed | tf_op | source)
XLA Modules:
  0.0 1079.9 jit_solution(13692981820854415552)
XLA Ops:
  38.4 5.1 fusion.129
  61.9 6.9 all-gather.8.cloned.1.call-done
  71.3 45.1 %while.48 = (s32[]{:T(128)}, f32[1,512,12]{1,2,0:T(8,128)}, f32[1,512,12]{1,2,0:T(8,128)}, f32[1,512,12,64]{1,3,2,0:T(8,128)}, bf16[1,1024,768]{1,2,0:T(8,128)(2...) while((s32[]{:T(128)}, f32[1,512,12]{1,2,0:T(8,128)}, ...), condition=%wide.region_5.0_spmd.clone, body=%wide.region_2.0_spmd.clone.sunk | while | flops 831688704 | bytes 100565304 | solution.py:64
  73.8 7.4 bitcast_reduce_fusion.2
  82.0 8.5 bitcast_add_fusion.12
  96.3 7.0 bitcast_reduce_fusion.2
  104.1 8.9 bitcast_add_fusion.12
  124.2 9.1 convert_reduce_fusion
  146.1 40.8 %while.49 = (s32[]{:T(128)}, f32[1,512,12,64]{1,3,2,0:T(8,128)}, bf16[1,1024,768]{1,2,0:T(8,128)(2,1)}, bf16[1,512,12,64]{1,3,2,0:T(8,128)(2,1)}, f32[1,512,12]{...) while((s32[]{:T(128)}, f32[1,512,12,64]{1,3,2,0:T(8,128)}, ...), condition=%wide.region_12.0_spmd.clone, body=%wide.region_11.0_spmd.clone.sunk | while | flops 1228013568 | bytes 41754864 | solution.py:64
  148.5 6.6 fusion.185
  155.2 11.3 %bitcast_add_fusion.13 = f32[1,512,12,64]{1,3,2,0:T(8,128)} fusion(f32[1,512,12,64]{1,3,2,0:T(8,128)} %get-tuple-element.1006, bf16[512,12,64]{0,2,1:T(8,128)(2,1)} %bitcast.364, f32[512,12]{0,1:T(8,128)} %bitcast.394, f32[512,12]{0,1:T(8,128)} %bitcast.384, f32[512,12]{0,1:T(8,128)} %bitcast.381, f32[12,512,512]{2,1,0:T(8,128)} %fusion.185, ...), kind=kOutput, calls=%fused_computation.30.clone.1 | convolution fusion | flops 825360384 | bytes 18161664 | tf_op jit(solution)/shard_map/while/body/eval_jaxpr/sqhk,skhd->sqhd/dot_general | solution.py:207
  168.9 6.3 fusion.185
  175.3 11.6 %bitcast_add_fusion.13 = f32[1,512,12,64]{1,3,2,0:T(8,128)} fusion(f32[1,512,12,64]{1,3,2,0:T(8,128)} %get-tuple-element.1006, bf16[512,12,64]{0,2,1:T(8,128)(2,1)} %bitcast.364, f32[512,12]{0,1:T(8,128)} %bitcast.394, f32[512,12]{0,1:T(8,128)} %bitcast.384, f32[512,12]{0,1:T(8,128)} %bitcast.381, f32[12,512,512]{2,1,0:T(8,128)} %fusion.185, ...), kind=kOutput, calls=%fused_computation.30.clone.1 | convolution fusion | flops 825360384 | bytes 18161664 | tf_op jit(solution)/shard_map/while/body/eval_jaxpr/sqhk,skhd->sqhd/dot_general | solution.py:207
  199.6 4.2 fusion.109
  203.9 52.4 %while.50 = (s32[]{:T(128)}, f32[1,512,12,64]{1,3,2,0:T(8,128)}, f32[1,512,12,64]{1,3,2,0:T(8,128)}, bf16[1,1024,12,64]{1,3,2,0:T(8,128)(2,1)}, bf16[1,512,12,64...) while((s32[]{:T(128)}, f32[1,512,12,64]{1,3,2,0:T(8,128)}, ...), condition=%wide.region_14.0_spmd.clone, body=%wide.region_13.0_spmd.clone.sunk | while | flops 1644036096 | bytes 49661728 | solution.py:64
  204.0 7.8 fusion.194
  213.0 7.3 bitcast_add_fusion.15
  220.3 9.5 bitcast_add_fusion.14
  229.9 7.8 fusion.194
  238.9 7.8 bitcast_add_fusion.15
  246.6 9.7 bitcast_add_fusion.14
  274.6 12.2 %convert_reduce_fusion.2 = (f32[768]{0:T(1024)}, f32[768]{0:T(1024)S(1)}, f32[768]{0:T(1024)S(1)}, bf16[1,512,768]{2,1,0:T(8,128)(2,1)}, bf16[1,512,768]{2,1,0:T(8,128)(2,1)}) fusion(f32[768]{0:T(1024)S(1)} %copy-done.73, f32[512]{0:T(512)S(1)} %bitcast.399, bf16[1,512,768]{2,1,0:T(8,128)(2,1)} %param.25, f32[512,768]{1,0:T(8,128)} %get-tuple-element.730, ...), kind=kOutput, calls=%fused_computation.119 | convolution fusion | flops 2442262272 | bytes 20493312 | tf_op jit(solution)/shard_map/dot_general | solution.py:168
  290.5 4.9 psum.77
  299.4 7.4 fusion.97
  307.5 8.9 fusion.122
  317.1 10.2 fusion.102
  327.4 6.4 reduce-scatter.8.cloned.1.call-done
  333.8 133.1 %reduce-scatter.14.cloned.1.call-done = f32[128,288]{0,1:T(8,128)} async-done(((f32[128,4608]{0,1:T(8,128)}), f32[128,288]{0,1:T(8,128)}) %reduce-scatter.14.cloned.1.call-update) | async-done | bytes 147472 | tf_op jit(solution)/shard_map/reduce_scatter | solution.py:327
  466.9 155.7 %reduce-scatter.6.cloned.1.call-done = f32[48,2304]{1,0:T(8,128)} async-done(((f32[768,2304]{1,0:T(8,128)}), f32[48,2304]{1,0:T(8,128)}) %reduce-scatter.6.cloned.1.call-update) | async-done | bytes 442384 | tf_op jit(solution)/shard_map/reduce_scatter | solution.py:320
  622.6 175.6 %reduce-scatter.10.cloned.1.call-done = f32[48,3072]{1,0:T(8,128)} async-done(((f32[768,3072]{1,0:T(8,128)}), f32[48,3072]{1,0:T(8,128)}) %reduce-scatter.10.cloned.1.call-update) | async-done | bytes 589840 | tf_op jit(solution)/shard_map/reduce_scatter | solution.py:323
  798.2 176.6 %reduce-scatter.12.cloned.1.call-done = f32[192,768]{1,0:T(8,128)} async-done(((f32[3072,768]{1,0:T(8,128)}), f32[192,768]{1,0:T(8,128)}) %reduce-scatter.12.cloned.1.call-update) | async-done | bytes 589840 | tf_op jit(solution)/shard_map/reduce_scatter | solution.py:325
  980.7 76.1 %all-reduce.9 = (f32[768]{0:T(1024)}, f32[768]{0:T(1024)}, f32[3072]{0:T(1024)}, f32[768]{0:T(1024)}, f32[4608]{0:T(1024)}) all-reduce(f32[768]{0:T(1024)S(1)} %copy-done.58, f32[768]{0:T(1024)} %get-tuple-element.614, f32[3072]{0:T(1024)S(1)} %copy-done.62, ...), channel_id=3, replica_groups=mesh['dp'=16,'ctx'=2] {'dp'}, use_global_device_ids=true, to_apply=%region_25.0.clone | all-reduce | flops 9984 | bytes 79872
  (321 shorter events, 153.0 us)
Async XLA Ops:
  7.2 52.1 %all-gather.6.cloned.1.call-start = ((), (), s32[]{:S(2)}) async-start(), calls=%async_computation.5 | async-start | bytes 2359296 | tf_op jit(solution)/shard_map/all_gather | solution.py:153
  10.9 126.2 %copy-start.52 = (f32[768]{0:T(1024)}, f32[768]{0:T(1024)S(1)}, u32[]{:S(2)}) copy-start(f32[768]{0:T(1024)S(1)} %get-tuple-element.625) | copy-start | bytes 9220
  43.5 25.2 %all-gather.8.cloned.1.call-start = ((), (), s32[]{:S(2)}) async-start(), calls=%async_computation.6 | async-start | bytes 2359296 | tf_op jit(solution)/shard_map/all_gather | solution.py:154
  46.0 157.9 %all-gather.10.cloned.1.call-start = ((), (), s32[]{:S(2)}) async-start(), calls=%async_computation.7 | async-start | bytes 2359296 | tf_op jit(solution)/shard_map/all_gather | solution.py:252
  52.4 151.5 %all-gather.12.cloned.1.call-start = ((), (), s32[]{:S(2)}) async-start(), calls=%async_computation.8 | async-start | bytes 2359296 | tf_op jit(solution)/shard_map/all_gather | solution.py:253
  56.0 81.0 %copy-start.50 = (f32[768]{0:T(1024)}, f32[768]{0:T(1024)S(1)}, u32[]{:S(2)}) copy-start(f32[768]{0:T(1024)S(1)} %convert_element_type.200) | copy-start | bytes 9220
  56.7 142.9 %copy-start.63 = (f32[1,512]{1,0:T(1,128)}, f32[1,512]{1,0:T(1,128)S(1)}, u32[]{:S(2)}) copy-start(f32[1,512]{1,0:T(1,128)S(1)} %convert_element_type.207) | copy-start | bytes 6148
  82.0 8.5 copy-start.1
  104.1 9.0 copy-start.1
  120.4 16.6 %copy-start.7 = (f32[1,512,768]{2,1,0:T(8,128)}, f32[1,512,768]{2,1,0:T(8,128)S(1)}, u32[]{:S(2)}) copy-start(f32[1,512,768]{2,1,0:T(8,128)S(1)} %get-tuple-element.701) | copy-start | bytes 4718596
  120.4 16.6 %copy-start.43 = (f32[512]{0:T(512)}, f32[512]{0:T(512)S(1)}, u32[]{:S(2)}) copy-start(f32[512]{0:T(512)S(1)} %broadcast_multiply_fusion.3) | copy-start | bytes 6148
  120.8 16.3 %copy-start.66 = (f32[512]{0:T(512)}, f32[512]{0:T(512)S(1)}, u32[]{:S(2)}) copy-start(f32[512]{0:T(512)S(1)} %fusion.115) | copy-start | bytes 6148
  124.2 9.2 copy-start.83
  138.1 61.5 %copy-start.68 = (f32[512]{0:T(512)}, f32[512]{0:T(512)S(1)}, u32[]{:S(2)}) copy-start(f32[512]{0:T(512)S(1)} %negate_multiply_fusion.1) | copy-start | bytes 6148
  146.0 187.8 %reduce-scatter.8.cloned.1.call-start = ((), (), s32[]{:S(2)}) async-start(), calls=%async_computation.10 | async-start | bytes 2506752 | tf_op jit(solution)/shard_map/reduce_scatter | solution.py:321
  148.5 6.6 copy-start.4
  168.9 6.3 copy-start.4
  203.8 263.1 %reduce-scatter.14.cloned.1.call-start = ((), (), s32[]{:S(2)}) async-start(), calls=%async_computation.13 | async-start | bytes 2506752 | tf_op jit(solution)/shard_map/reduce_scatter | solution.py:327
  203.9 7.8 copy-start.30
  204.0 7.8 copy-start.31
  204.0 8.4 copy-start.29
  229.8 7.8 copy-start.30
  229.8 7.8 copy-start.31
  229.8 8.4 copy-start.29
  274.6 12.8 %copy-start.49 = (f32[768]{0:T(1024)S(1)}, f32[768]{0:T(1024)}, u32[]{:S(2)}) copy-start(f32[768]{0:T(1024)} %reduce_sum.248) | copy-start | bytes 9220
  274.6 13.3 %copy-start.70 = (f32[768]{0:T(1024)S(1)}, f32[768]{0:T(1024)}, u32[]{:S(2)}) copy-start(f32[768]{0:T(1024)} %get-tuple-element.616) | copy-start | bytes 9220
  298.8 323.8 %reduce-scatter.6.cloned.1.call-start = ((), (), s32[]{:S(2)}) async-start(), calls=%async_computation.9 | async-start | bytes 7520256 | tf_op jit(solution)/shard_map/reduce_scatter | solution.py:320
  306.8 491.4 %reduce-scatter.10.cloned.1.call-start = ((), (), s32[]{:S(2)}) async-start(), calls=%async_computation.11 | async-start | bytes 10027008 | tf_op jit(solution)/shard_map/reduce_scatter | solution.py:323
  316.4 658.4 %reduce-scatter.12.cloned.1.call-start = ((), (), s32[]{:S(2)}) async-start(), calls=%async_computation.12 | async-start | bytes 10027008 | tf_op jit(solution)/shard_map/reduce_scatter | solution.py:325
  327.3 653.3 %copy-start.58 = (f32[768]{0:T(1024)S(1)}, f32[768]{0:T(1024)}, u32[]{:S(2)}) copy-start(f32[768]{0:T(1024)} %get-tuple-element.617) | copy-start | bytes 9220
  327.4 653.3 %copy-start.62 = (f32[3072]{0:T(1024)S(1)}, f32[3072]{0:T(1024)}, u32[]{:S(2)}) copy-start(f32[3072]{0:T(1024)} %get-tuple-element.734) | copy-start | bytes 36868
  327.4 739.7 %all-reduce.14.cloned.1.call-start = ((), (), s32[]{:S(2)}) async-start(), calls=%async_computation.14 | async-start | bytes 3833856 | tf_op jit(solution)/shard_map/psum | solution.py:330
  (73 other events, 195.5 us)
Sparse Core Ops, SparseCore 0:
  43.6 12.4 all-gather.5
  57.7 10.9 all-gather.7
  70.3 10.9 all-gather.9
  146.2 10.9 all-gather.11
  203.9 129.8 reduce-scatter.7
  339.3 127.5 reduce-scatter.13
  472.3 150.2 reduce-scatter.5
  628.3 169.8 reduce-scatter.9
  804.8 169.9 reduce-scatter.11
  977.3 20.2 all-reduce.13
where the time goes:
time: 1090 us; the launch traced here: 1080 us
  waiting for transfers between devices  654 us (60%)
  matrix products  190 us (17%)
  blocking collectives  94.7 us (9%)
  local copies, waits for them, and re-layouts  74.8 us (7%)
  other arithmetic  47.2 us (4%)
  between operations  17 us (2%)
    reduce_scatter x1, waiting for transfers between devices, local(): lax.psum_scatter(grad_fc2, 'dp', scatter_dimension=0, tiled=True)  177 us
    reduce_scatter x1, waiting for transfers between devices, local(): lax.psum_scatter(grad_fc1, 'dp', scatter_dimension=0, tiled=True)  176 us
    reduce_scatter x1, waiting for transfers between devices, local(): lax.psum_scatter(grad_qkv, 'dp', scatter_dimension=0, tiled=True)  156 us
    reduce_scatter x1, waiting for transfers between devices, local(): lax.psum_scatter(grad_ada, 'dp', scatter_dimension=1, tiled=True)  133 us
    unnamed x1, blocking collectives  76.1 us
    unnamed x168, local copies, waits for them, and re-layouts  29.7 us
    dot_general x4, matrix products, score_grads(): jnp.einsum('sqhd,skhd->sqhk', query_blk, key_blk, preferred_element_type=...  28.5 us
    dot_general x2, matrix products, query_only_step(): jnp.einsum('sqhk,skhd->sqhd', grad_scores, key_blk, preferred_element_typ...  22.9 us
  transfers between devices with their start and end apart: 10, of which 6 were waited for; matrix products, arithmetic and copies ran while one was open for 24% of the time, Pallas kernels for 0%

commit v1 on v0

--- a/solution.py
+++ b/solution.py
@@ -1,15 +1,438 @@
+import functools
+
 import jax
 import jax.numpy as jnp
 from jax import lax
+from jax.experimental import pallas as pl
+from jax.experimental.pallas import tpu as pltpu
 from jax.sharding import PartitionSpec as P
 
 HEADS = 12
 HEAD_DIM = 64
-
-
 EPS = 1e-05
 SCORE_SCALE = 0.125
 NEG_START = -1e30
+
+def mask_half(value, head):
+    lane = lax.broadcasted_iota(jnp.int32, value.shape, 1)
+    keep = (lane < HEAD_DIM) if head == 0 else (lane >= HEAD_DIM)
+    return jnp.where(keep, value, jnp.zeros_like(value))
+
+
+def attn_fwd_body(q_ref, k_ref, v_ref, out_ref, prob_ref, inv_ref, km_ref, vt_ref):
+    @pl.when(pl.program_id(1) == 0)
+    def _():
+        keys = k_ref[...]
+        for head in (0, 1):
+            km_ref[head] = mask_half(keys, head)
+        vt_ref[...] = v_ref[...].T
+
+    queries = q_ref[...]
+    for head in (0, 1):
+        rows = slice(head * HEAD_DIM, (head + 1) * HEAD_DIM)
+        scores = lax.dot_general(
+            km_ref[head], queries, (((1,), (1,)), ((), ())), preferred_element_type=jnp.float32
+        )
+        top = jnp.max(scores, axis=0, keepdims=True)
+        raised = jnp.exp(scores - top)
+        total = jnp.sum(raised, axis=0, keepdims=True)
+        prob = raised.astype(jnp.bfloat16)
+        prob_ref[head] = prob
+        inverse = 1.0 / total
+        inv_ref[0, head : head + 1, :] = inverse
+        part = jnp.dot(vt_ref[rows, :], prob, preferred_element_type=jnp.float32)
+        out_ref[rows, :] = (part * inverse).astype(jnp.bfloat16)
+
+
+def attn_fwd(queries, keys, values, blk):
+    length, width = keys.shape
+    pairs = width // 128
+    nq = queries.shape[0]
+    return pl.pallas_call(
+        attn_fwd_body,
+        grid=(pairs, nq // blk),
+        in_specs=[
+            pl.BlockSpec((blk, 128), lambda p, i: (i, p)),
+            pl.BlockSpec((length, 128), lambda p, i: (0, p)),
+            pl.BlockSpec((length, 128), lambda p, i: (0, p)),
+        ],
+        out_specs=[
+            pl.BlockSpec((128, blk), lambda p, i: (p, i)),
+            pl.BlockSpec((2, length, blk), lambda p, i: (p, 0, i)),
+            pl.BlockSpec((1, 8, blk), lambda p, i: (p, 0, i)),
+        ],
+        out_shape=[
+            jax.ShapeDtypeStruct((width, nq), jnp.bfloat16),
+            jax.ShapeDtypeStruct((2 * pairs, length, nq), jnp.bfloat16),
+            jax.ShapeDtypeStruct((pairs, 8, nq), jnp.float32),
+        ],
+        scratch_shapes=[
+            pltpu.VMEM((2, length, 128), jnp.bfloat16),
+            pltpu.VMEM((128, length), jnp.bfloat16),
+        ],
+        compiler_params=pltpu.CompilerParams(vmem_limit_bytes=48 << 20),
+        cost_estimate=pl.CostEstimate(
+            flops=8 * nq * length * width, bytes_accessed=nq * length * 4 * pairs, transcendentals=0
+        ),
+    )(queries, keys, values)
+
+
+def attn_bwd_body(
+    prob_ref, inv_ref, gt_ref, out_ref, q_ref, k_ref, v_ref,
+    dq_ref, dk_ref, dv_ref, vm_ref, kt_ref, dk_acc, dv_acc,
+):
+    step = pl.program_id(1)
+
+    @pl.when(step == 0)
+    def _():
+        values = v_ref[...]
+        for head in (0, 1):
+            vm_ref[head] = mask_half(values, head)
+        kt_ref[...] = k_ref[...].T
+
+    queries = q_ref[...]
+    grad_t = gt_ref[...].astype(jnp.float32)
+    blk = grad_t.shape[1]
+    row_id = lax.broadcasted_iota(jnp.int32, (128, blk), 0)
+    inverse = jnp.where(row_id < HEAD_DIM, inv_ref[0, 0:1, :], inv_ref[0, 1:2, :])
+    grad_t = grad_t * inverse
+    product = grad_t * out_ref[...].astype(jnp.float32)
+    grad_b = grad_t.astype(jnp.bfloat16)
+    dk_new = None
+    for head in (0, 1):
+        rows = slice(head * HEAD_DIM, (head + 1) * HEAD_DIM)
+        delta = jnp.sum(product[rows], axis=0, keepdims=True)
+        keep = (row_id < HEAD_DIM) if head == 0 else (row_id >= HEAD_DIM)
+        grad_m = jnp.where(keep, grad_b, jnp.zeros_like(grad_b))
+        grad_p = jnp.dot(vm_ref[head], grad_b, preferred_element_type=jnp.float32)
+        prob = prob_ref[head]
+        grad_s = (prob.astype(jnp.float32) * (grad_p - delta)).astype(jnp.bfloat16)
+        dv_h = lax.dot_general(
+            prob, grad_m, (((1,), (1,)), ((), ())), preferred_element_type=jnp.float32
+        )
+        dk_h = jnp.dot(grad_s, mask_half(queries, head), preferred_element_type=jnp.float32)
+        if dk_new is None:
+            dk_new, dv_new = dk_h, dv_h
+        else:
+            dk_new, dv_new = dk_new + dk_h, dv_new + dv_h
+        dq_t = jnp.dot(kt_ref[rows, :], grad_s, preferred_element_type=jnp.float32)
+        dq_ref[rows, :] = dq_t * SCORE_SCALE
+
+    @pl.when(step == 0)
+    def _():
+        dk_acc[...] = dk_new
+        dv_acc[...] = dv_new
+
+    @pl.when(step > 0)
+    def _():
+        dk_acc[...] += dk_new
+        dv_acc[...] += dv_new
+
+    @pl.when(step == pl.num_programs(1) - 1)
+    def _():
+        dk_ref[...] = dk_acc[...]
+        dv_ref[...] = dv_acc[...].astype(jnp.bfloat16)
+
+
+def attn_bwd(prob, inverse, grad_t, out_t, queries, keys, values, blk):
+    length, width = keys.shape
+    pairs = width // 128
+    nq = queries.shape[0]
+    return pl.pallas_call(
+        attn_bwd_body,
+        grid=(pairs, nq // blk),
+        in_specs=[
+            pl.BlockSpec((2, length, blk), lambda p, i: (p, 0, i)),
+            pl.BlockSpec((1, 8, blk), lambda p, i: (p, 0, i)),
+            pl.BlockSpec((128, blk), lambda p, i: (p, i)),
+            pl.BlockSpec((128, blk), lambda p, i: (p, i)),
+            pl.BlockSpec((blk, 128), lambda p, i: (i, p)),
+            pl.BlockSpec((length, 128), lambda p, i: (0, p)),
+            pl.BlockSpec((length, 128), lambda p, i: (0, p)),
+        ],
+        out_specs=[
+            pl.BlockSpec((128, blk), lambda p, i: (p, i)),
+            pl.BlockSpec((length, 128), lambda p, i: (0, p)),
+            pl.BlockSpec((length, 128), lambda p, i: (0, p)),
+        ],
+        out_shape=[
+            jax.ShapeDtypeStruct((width, nq), jnp.float32),
+            jax.ShapeDtypeStruct((length, width), jnp.float32),
+            jax.ShapeDtypeStruct((length, width), jnp.bfloat16),
+        ],
+        scratch_shapes=[
+            pltpu.VMEM((2, length, 128), jnp.bfloat16),
+            pltpu.VMEM((128, length), jnp.bfloat16),
+            pltpu.VMEM((length, 128), jnp.float32),
+            pltpu.VMEM((length, 128), jnp.float32),
+        ],
+        compiler_params=pltpu.CompilerParams(vmem_limit_bytes=48 << 20),
+        cost_estimate=pl.CostEstimate(
+            flops=16 * nq * length * width, bytes_accessed=nq * length * 4 * pairs, transcendentals=0
+        ),
+    )(prob, inverse, grad_t, out_t, queries, keys, values)
+
+
+def layer_stats(stream):
+    row_mean = jnp.mean(stream, axis=-1, keepdims=True)
+    centred = stream - row_mean
+    variance = jnp.mean(centred * centred, axis=-1, keepdims=True)
+    inv = lax.rsqrt(variance + EPS)
+    return centred * inv, inv
+
+
+def tables(positions):
+    inv_freq = 10000.0 ** (-jnp.arange(0, HEAD_DIM, 2).astype(jnp.float32) / HEAD_DIM)
+    angles = positions.astype(jnp.float32)[:, None] * inv_freq
+    cos_t, sin_t = jnp.cos(angles), jnp.sin(angles)
+    return jnp.concatenate([cos_t, cos_t], -1), jnp.concatenate([-sin_t, sin_t], -1)
+
+
+def swap_halves(x):
+    rows, width = x.shape
+    half = HEAD_DIM // 2
+    lane = lax.broadcasted_iota(jnp.int32, x.shape, 1) % HEAD_DIM
+    return jnp.where(lane < half, jnp.roll(x, -half, 1), jnp.roll(x, half, 1))
+
+
+def dot(a, b):
+    return jnp.dot(a, b, preferred_element_type=jnp.float32)
+
+
+def dot_tn(a, b):
+    return lax.dot_general(a, b, (((0,), (0,)), ((), ())), preferred_element_type=jnp.float32)
+
+
+def dot_nt(a, b):
+    return lax.dot_general(a, b, (((1,), (1,)), ((), ())), preferred_element_type=jnp.float32)
+
+
+class Grid:
+    def __init__(self, ndp):
+        self.nz = ndp // 4
+        self.me = lax.axis_index("dp")
+        self.x = self.me % 2
+        self.y = (self.me // 2) % 2
+        self.z = self.me // 4
+        self.px = [(i, i ^ 1) for i in range(ndp)]
+        self.py = [(i, i ^ 2) for i in range(ndp)]
+        self.pz = [[(i, (i + 4 * k) % ndp) for i in range(ndp)] for k in range(self.nz)]
+
+    def pick(self, arr, index, axis):
+        return lax.dynamic_index_in_dim(arr, index, axis, keepdims=False)
+
+    def reduce(self, grad):
+        rows, cols = grad.shape
+        r = rows // (4 * self.nz)
+        g = grad.reshape(self.nz, 2, 2, r, cols)
+        h = cols // 2
+        ga, gb = g[..., :h], g[..., h:]
+        ra = lax.ppermute(self.pick(ga, 1 - self.x, 2), "dp", self.px)
+        rb = lax.ppermute(self.pick(gb, 1 - self.y, 1), "dp", self.py)
+        ha = self.pick(ga, self.x, 2) + ra
+        hb = self.pick(gb, self.y, 1) + rb
+        ra = lax.ppermute(self.pick(ha, 1 - self.y, 1), "dp", self.py)
+        rb = lax.ppermute(self.pick(hb, 1 - self.x, 1), "dp", self.px)
+        ja = self.pick(ha, self.y, 1) + ra
+        jb = self.pick(hb, self.x, 1) + rb
+        j = jnp.concatenate([ja, jb], axis=-1)
+        total = self.pick(j, self.z, 0).astype(jnp.float32)
+        for k in range(1, self.nz):
+            got = lax.ppermute(self.pick(j, (self.z + k) % self.nz, 0), "dp", self.pz[k])
+            total = total + got.astype(jnp.float32)
+        return total
+
+    def spread(self, mine):
+        n = mine.shape[-1]
+        m = mine.reshape(self.nz, 2, 2, n)
+        got = lax.ppermute(self.pick(m, 1 - self.x, 2), "dp", self.px)
+        m = jnp.stack([self.pick(m, self.x, 2), got], 0)
+        got = lax.ppermute(self.pick(m, 1 - self.y, 2), "dp", self.py)
+        m = jnp.stack([self.pick(m, self.y, 2), got], 0)
+        parts = [self.pick(m, self.z, 2)]
+        for k in range(1, self.nz):
+            parts.append(
+                lax.ppermute(self.pick(m, (self.z + k) % self.nz, 2), "dp", self.pz[k])
+            )
+        return jnp.stack(parts, 0).reshape(4 * self.nz, n)
+
+
+def local_pair(
+    tokens_in, cond_vec, positions, absorbed, cotangent, norm1_gain, qkv_weight, out_weight,
+    norm2_gain, fc1_weight, fc1_bias, fc2_weight, fc2_bias, ada_weight, ada_bias, *, ndp,
+):
+    f32, bf16 = jnp.float32, jnp.bfloat16
+    _, span, width = tokens_in.shape
+    ff = fc1_weight.shape[1]
+    hw, hf = width // 2, ff // 2
+    core = lax.axis_index("ctx")
+    grid = Grid(ndp)
+    swap = lambda v: lax.ppermute(v, "ctx", [(0, 1), (1, 0)])
+
+    tok = tokens_in[0]
+    weighted_b = cotangent[0] * absorbed[0].astype(bf16)[:, None]
+    tok_all = jnp.concatenate([tok, swap(tok)], 0)
+    wtd_all = jnp.concatenate([weighted_b, swap(weighted_b)], 0)
+    pos_all = jnp.concatenate([positions[0], swap(positions[0])], 0)
+
+    modulation = dot(cond_vec, ada_weight) + ada_bias.astype(f32)
+    shift_one, scale_one, gate_one, shift_two, scale_two, gate_two = jnp.split(modulation, 6, -1)
+    gain_one = norm1_gain.astype(f32)[None]
+    gain_two = norm2_gain.astype(f32)[None]
+    stream = tok_all.astype(f32)
+    a_one, inv_one = layer_stats(stream)
+    normed_one = (a_one * gain_one * (1.0 + scale_one) + shift_one).astype(bf16)
+
+    def cols(w, start, n):
+        return lax.dynamic_slice_in_dim(w, start, n, 1)
+
+    def rows(w, start, n):
+        return lax.dynamic_slice_in_dim(w, start, n, 0)
+
+    w_q = cols(qkv_weight, core * hw, hw)
+    w_k = cols(qkv_weight, width + core * hw, hw)
+    w_v = cols(qkv_weight, 2 * width + core * hw, hw)
+    cos_t, sin_t = tables(pos_all)
+    cos_w = jnp.tile(cos_t, (1, hw // HEAD_DIM))
+    sin_w = jnp.tile(sin_t, (1, hw // HEAD_DIM))
+    q_pre, k_pre = dot(normed_one, w_q), dot(normed_one, w_k)
+    queries = (SCORE_SCALE * (q_pre * cos_w + swap_halves(q_pre) * sin_w)).astype(bf16)
+    keys = (k_pre * cos_w + swap_halves(k_pre) * sin_w).astype(bf16)
+    values = dot(normed_one, w_v).astype(bf16)
+
+    att_t, prob, inverse = attn_fwd(queries, keys, values, 512)
+    att_other = swap(att_t[:, span:])
+    w_o_mine = rows(out_weight, core * hw, hw)
+    w_o_other = rows(out_weight, (1 - core) * hw, hw)
+    branch_att = dot_tn(att_t[:, :span], w_o_mine) + dot_tn(att_other, w_o_other)
+    middle = stream[:span] + gate_one * branch_att
+    a_two, inv_two = layer_stats(middle)
+    normed_two = (a_two * gain_two * (1.0 + scale_two) + shift_two).astype(bf16)
+    n2_all = jnp.concatenate([normed_two, swap(normed_two)], 0)
+
+    w1 = cols(fc1_weight, core * hf, hf)
+    b1 = lax.dynamic_slice_in_dim(fc1_bias, core * hf, hf, 0).astype(f32)
+    w2 = rows(fc2_weight, core * hf, hf)
+    hidden_pre = dot(n2_all, w1) + b1
+    c0 = 0.7978845608028654
+    th = jnp.tanh(c0 * (hidden_pre + 0.044715 * hidden_pre * hidden_pre * hidden_pre))
+    hidden = (0.5 * hidden_pre * (1.0 + th)).astype(bf16)
+    slope = 0.5 * (1.0 + th) + 0.5 * hidden_pre * (1.0 - th * th) * c0 * (
+        1.0 + 3 * 0.044715 * hidden_pre * hidden_pre
+    )
+    wtd = wtd_all.astype(f32)
+    g_mlp = (wtd * gate_two).astype(bf16)
+    grad_pre = (dot_nt(g_mlp, w2) * slope).astype(bf16)
+    grad_fc1 = dot_tn(n2_all, grad_pre).astype(bf16)
+    red_fc1 = grid.reduce(grad_fc1)
+    grad_fc2 = dot_tn(hidden, g_mlp).astype(bf16)
+    keep2 = cols(grad_fc2, core * hw, hw)
+    got2 = swap(cols(grad_fc2, (1 - core) * hw, hw))
+    low2 = jnp.where(core == 0, keep2, got2)
+    high2 = jnp.where(core == 0, got2, keep2)
+    red_fc2 = grid.reduce(jnp.concatenate([low2, high2], 0))
+    sum_fc2b = jnp.sum(g_mlp.astype(f32), axis=0)
+    sum_fc1b = jnp.sum(grad_pre.astype(f32), axis=0)
+    part_mlp = dot(hidden, w2)
+    g_gate_two = jnp.sum(wtd * part_mlp, axis=0) + fc2_bias.astype(f32) * jnp.sum(wtd[:span], axis=0)
+    branch_mlp = part_mlp[:span] + swap(part_mlp[span:].astype(bf16)).astype(f32) + fc2_bias.astype(f32)
+    mixed = (middle + gate_two * branch_mlp).astype(bf16)
+    part_n2 = dot_nt(grad_pre, w1)
+    g_n2 = part_n2[:span] + swap(part_n2[span:].astype(bf16)).astype(f32)
+
+    g_shift_two = jnp.sum(g_n2, axis=0)
+    sum_ga_two = jnp.sum(g_n2 * a_two, axis=0)
+    ga = g_n2 * gain_two * (1.0 + scale_two)
+    g_mid = wtd[:span] + inv_two * (
+        ga - jnp.mean(ga, -1, keepdims=True) - a_two * jnp.mean(ga * a_two, -1, keepdims=True)
+    )
+    g_gate_one = jnp.sum(g_mid * branch_att, axis=0)
+    g_att = (g_mid * gate_one).astype(bf16)
+    g_att_all = jnp.concatenate([g_att, swap(g_att)], 0)
+    g_attn_t = dot_nt(w_o_mine, g_att_all).astype(bf16)
+    grad_out = dot(att_t, g_att_all).astype(bf16)
+    keep_o = cols(grad_out, core * hw, hw)
+    got_o = swap(cols(grad_out, (1 - core) * hw, hw))
+    low_o = jnp.where(core == 0, keep_o, got_o)
+    high_o = jnp.where(core == 0, got_o, keep_o)
+    red_out = grid.reduce(jnp.concatenate([low_o, high_o], 0))
+
+    dq_t, dk, dv = attn_bwd(prob, inverse, g_attn_t, att_t, queries, keys, values, 512)
+    dq = dq_t.T
+    g_q = (dq * cos_w - swap_halves(dq) * sin_w).astype(bf16)
+    g_k = (dk * cos_w - swap_halves(dk) * sin_w).astype(bf16)
+    g_qkv = jnp.concatenate([g_q, g_k, dv], 1)
+    grad_qkv = dot_tn(normed_one, g_qkv).astype(bf16)
+    red_qkv = grid.reduce(grad_qkv)
+    w_qkv = jnp.concatenate([w_q, w_k, w_v], 1)
+    part_n1 = dot_nt(g_qkv, w_qkv)
+    g_n1 = part_n1[:span] + swap(part_n1[span:].astype(bf16)).astype(f32)
+    a_own = a_one[:span]
+    g_shift_one = jnp.sum(g_n1, axis=0)
+    sum_ga_one = jnp.sum(g_n1 * a_own, axis=0)
+    ga = g_n1 * gain_one * (1.0 + scale_one)
+    input_grad = (
+        g_mid
+        + inv_one[:span]
+        * (ga - jnp.mean(ga, -1, keepdims=True) - a_own * jnp.mean(ga * a_own, -1, keepdims=True))
+    ).astype(bf16)
+
+    vec = jnp.stack(
+        [
+            g_shift_one, sum_ga_one * gain_one[0], g_gate_one,
+            g_shift_two, sum_ga_two * gain_two[0], g_gate_two,
+            sum_ga_one * (1.0 + scale_one[0]), sum_ga_two * (1.0 + scale_two[0]),
+        ]
+    )
+    vec = vec + swap(vec)
+    g_mod = vec[:6].reshape(1, 6 * width)
+    cond_grad = lax.dot_general(
+        g_mod, ada_weight.astype(f32), (((1,), (1,)), ((), ())),
+        precision=lax.Precision.HIGHEST, preferred_element_type=f32,
+    )
+    other_b1 = swap(sum_fc1b)
+    fc1b = jnp.where(
+        core == 0, jnp.concatenate([sum_fc1b, other_b1]), jnp.concatenate([other_b1, sum_fc1b])
+    )
+    na, nb, nc = 6 * width // ndp, width // ndp, ff // ndp
+    small = jnp.concatenate(
+        [
+            g_mod.reshape(ndp, na), vec[6].reshape(ndp, nb), vec[7].reshape(ndp, nb),
+            sum_fc2b.reshape(ndp, nb), fc1b.reshape(ndp, nc),
+        ],
+        axis=1,
+    )
+    got = grid.spread(small)
+    cond_all = grid.spread(jnp.broadcast_to(cond_vec.astype(f32), (ndp, cond_vec.shape[1])))
+    ada_grad = lax.dot_general(
+        cond_all, got[:, :na], (((0,), (0,)), ((), ())),
+        precision=lax.Precision.HIGHEST, preferred_element_type=f32,
+    )
+    sums = jnp.sum(got, axis=0)
+    ada_bias_grad = sums[:na]
+    norm1_grad = sums[na : na + nb]
+    norm2_grad = sums[na + nb : na + 2 * nb]
+    fc2_bias_grad = sums[na + 2 * nb : na + 3 * nb]
+    fc1_bias_grad = sums[na + 3 * nb :]
+
+    def both(mine):
+        mine_b = mine.astype(bf16)
+        other = swap(mine_b)
+        low = jnp.where(core == 0, mine_b, other).astype(f32)
+        high = jnp.where(core == 0, other, mine_b).astype(f32)
+        return low, high
+
+    fc1_grad = jnp.concatenate(both(red_fc1), 1)
+    fc2_grad = jnp.concatenate(both(red_fc2), 1)
+    out_grad = jnp.concatenate(both(red_out), 1)
+    lo, hi = both(red_qkv)
+    qkv_grad = jnp.concatenate(
+        [lo[:, :hw], hi[:, :hw], lo[:, hw : 2 * hw], hi[:, hw : 2 * hw], lo[:, 2 * hw :], hi[:, 2 * hw :]], 1
+    )
+    return (
+        mixed[None], input_grad[None], cond_grad, norm1_grad, qkv_grad, out_grad, norm2_grad,
+        fc1_grad, fc1_bias_grad, fc2_grad, fc2_bias_grad, ada_grad, ada_bias_grad,
+    )
 
 
 def layer_norm(stream):
@@ -77,7 +500,7 @@
     return (probability, grad_scores)
 
 
-def local(
+def local_any(
     tokens_in,
     cond_vec,
     positions,
@@ -345,6 +768,13 @@
     return (mixed, input_grad, cond_grad) + tuple(summed)
 
 
+def local(*args, ndp, nctx):
+    seqs, span, _ = args[0].shape
+    if nctx == 2 and seqs == 1 and ndp % 4 == 0 and span % 256 == 0:
+        return local_pair(*args, ndp=ndp)
+    return local_any(*args)
+
+
 def solution(mesh):
     in_specs = (
         P("dp", "ctx", None),
@@ -378,4 +808,5 @@
         P(None, "dp"),
         P("dp"),
     )
-    return jax.shard_map(local, mesh=mesh, in_specs=in_specs, out_specs=out_specs, check_vma=False)
+    step = functools.partial(local, ndp=mesh.shape["dp"], nctx=mesh.shape["ctx"])
+    return jax.shard_map(step, mesh=mesh, in_specs=in_specs, out_specs=out_specs, check_vma=False)

time: 1090 us -> 319 us (0.29)
  waiting for transfers between devices: 654 us -> 52 us
  matrix products: 190 us -> 60.1 us
  blocking collectives: 94.7 us -> 0 us
  starting transfers between devices: 1.11 us -> 66 us
  Pallas kernels: 0 us -> 32.5 us
  local copies, waits for them, and re-layouts: 74.8 us -> 48.6 us
  between operations: 17 us -> 2.84 us
    reduce_scatter x5 -> x0, waiting for transfers between devices: 647 us -> none  [the longest x1 177 us: local(): lax.psum_scatter(grad_fc2, 'dp', scatter_dimension=0, tiled=True)]
    dot_general x28 -> x18, matrix products: 190 us -> 60.1 us  [the longest x4 21.7 us: dot_nt(): lax.dot_general(a, b, (((1,), (1,)), ((), ())), preferred_element_type=jn...]
    unnamed x1 -> x0, blocking collectives: 76.1 us -> none
    ppermute x0 -> x55, starting transfers between devices: none -> 66 us  [the longest x12 27.5 us: reduce(): lax.ppermute(self.pick(j, (self.z + k) % self.nz, 0), 'dp', self.pz[k])]
    ppermute x0 -> x55, waiting for transfers between devices: none -> 52 us  [the longest x12 15.4 us: reduce(): lax.ppermute(self.pick(j, (self.z + k) % self.nz, 0), 'dp', self.pz[k])]
    pallas_call x0 -> x2, Pallas kernels: none -> 32.5 us  [the longest x1 17.5 us: attn_bwd(): pl.pallas_call(attn_bwd_body, grid=(pairs, nq // blk), in_specs=[pl.Block...]
    unnamed x168 -> x200, local copies, waits for them, and re-layouts: 29.7 us -> 10.4 us
    another operation x0 -> x12, local copies, waits for them, and re-layouts: none -> 11.4 us  [the longest x2 4.38 us: local_pair(): cos_w = jnp.tile(cos_t, (1, hw // HEAD_DIM))]
  transfers between devices with their start and end apart: 10 -> 55, of which waited for: 6 -> 19; matrix products, arithmetic and copies ran while one was open for 24% -> 42% of each run, Pallas kernels for 0% -> 10%
where the time goes in v1:
time: 319 us; the launch traced here: 315 us
  starting transfers between devices  66 us (21%)
  matrix products  60.1 us (19%)
  other arithmetic  52.6 us (16%)
  waiting for transfers between devices  52 us (16%)
  local copies, waits for them, and re-layouts  48.6 us (15%)
  Pallas kernels  32.5 us (10%)
    ppermute x12, starting transfers between devices, reduce(): lax.ppermute(self.pick(j, (self.z + k) % self.nz, 0), 'dp', self.pz[k])  27.5 us
    dot_general x4, matrix products, dot_nt(): lax.dot_general(a, b, (((1,), (1,)), ((), ())), preferred_element_type=jn...  21.7 us
    dot_general x5, matrix products, dot_tn(): lax.dot_general(a, b, (((0,), (0,)), ((), ())), preferred_element_type=jn...  18.2 us
    dot_general x7, matrix products, dot(): return jnp.dot(a, b, preferred_element_type=jnp.float32)  17.6 us
    pallas_call x1, Pallas kernels, attn_bwd(): pl.pallas_call(attn_bwd_body, grid=(pairs, nq // blk), in_specs=[pl.Block...  17.5 us
    ppermute x12, waiting for transfers between devices, reduce(): lax.ppermute(self.pick(j, (self.z + k) % self.nz, 0), 'dp', self.pz[k])  15.4 us
    pallas_call x1, Pallas kernels, attn_fwd(): pl.pallas_call(attn_fwd_body, grid=(pairs, nq // blk), in_specs=[pl.Block...  15.1 us
    ppermute x6, starting transfers between devices, spread(): lax.ppermute(self.pick(m, (self.z + k) % self.nz, 2), 'dp', self.pz[k])  11.3 us
  transfers between devices with their start and end apart: 55, of which 19 were waited for; matrix products, arithmetic and copies ran while one was open for 42% of the time, Pallas kernels for 10%

profile of v1, /device:TPU:0, one launch (start us, length us, event | category | flops | bytes accessed | tf_op | source)
XLA Modules:
  0.0 314.6 jit_solution(6966594305486178571)
XLA Ops:
  8.5 2.8 constant_dynamic-slice_fusion.16
  13.3 3.0 copy.94
  17.7 3.0 copy.99
  21.7 3.4 %subtract_multiply_fusion = (f32[1024,768]{1,0:T(8,128)}, bf16[1024,768]{1,0:T(8,128)(2,1)S(1)}) fusion(f32[1024]{0:T(1024)S(1)} %add_rsqrt_fusion, f32[1024]{0:T(1024)S(1)} %broadcast_multiply_fusion, bf16[512,768]{1,0:T(8,128)(2,1)S(1)} %collective-permute-done, bf16[512,768]{1,0:T(8,128)(2,1)S(1)} %bitcast.224, f32[768]{0:T(1024)S(1)} %get-tuple-element.40, ...), kind=kLoop, calls=%fused_computation.19 | loop fusion | flops 7864320 | bytes 6308864 | tf_op jit(solution)/shard_map/mul | solution.py:181
  32.3 15.1 %shard_map.246 = (bf16[384,1024]{1,0:T(8,128)(2,1)S(1)}, bf16[6,1024,1024]{2,1,0:T(8,128)(2,1)}, f32[3,8,1024]{2,1,0:T(8,128)S(1)}) custom-call(bf16[1024,384]{1,0:T(8,128)(2,1)S(1)} %get-tuple-element.57.q_ref, bf16[1024,384]{1,0:T(8,128)(2,1)S(1)} %get-tuple-element.56.k_ref, bf16[1024,384]{1,0:T(8,128)(2,1)S(1)} %convolution_convert_fusion.4.v_ref), custom_call_target="tpu_custom_call" | custom-call | flops 3221225472 | bytes 12582912 | tf_op jit(solution)/shard_map/pallas_call | solution.py:51
  53.1 2.9 collective-permute-start.50
  66.8 2.6 collective-permute-start.53
  75.1 3.4 %maximum_convert_fusion = f32[1024,768]{1,0:T(8,128)} fusion(bf16[512,768]{1,0:T(8,128)(2,1)} %collective-permute-done.5, bf16[512,768]{1,0:T(8,128)(2,1)} %bitcast_multiply_fusion), kind=kLoop, calls=%fused_computation.58 | loop fusion | flops 3145728 | bytes 4718592 | tf_op jit(solution)/shard_map/convert_element_type | solution.py:323
  78.5 4.8 %fusion.12 = f32[1024,1536]{1,0:T(8,128)S(1)} fusion(bf16[768,3072]{1,0:T(8,128)(2,1)} %param.24, s32[]{:T(128)S(6)} %select_n.310, bf16[512,768]{1,0:T(8,128)(2,1)} %collective-permute-done.3, bf16[512,768]{1,0:T(8,128)(2,1)} %add_convert_fusion.2), kind=kOutput, calls=%fused_computation.28 | convolution fusion | flops 2419064832 | bytes 10223620 | tf_op jit(solution)/shard_map/dot_general | solution.py:199
  83.4 10.6 %convert_reduce_fusion = (f32[1536]{0:T(1024)}, bf16[1024,1536]{1,0:T(8,128)(2,1)}) fusion(f32[1024,1536]{1,0:T(8,128)S(1)} %fusion.12, f32[1536]{0:T(1024)S(1)} %dynamic-slice_convert_fusion, bf16[3072,768]{1,0:T(8,128)(2,1)S(1)} %bitcast.251, s32[]{:T(128)S(6)} %select_n.310, f32[768]{0:T(1024)S(1)} %copy-done.68, ...), kind=kOutput, calls=%fused_computation.9 | convolution fusion | flops 2455239168 | bytes 13387780 | tf_op jit(solution)/shard_map/dot_general | solution.py:207
  95.3 7.4 %convolution_convert_fusion = bf16[1536,768]{1,0:T(8,128)(2,1)S(1)} fusion(f32[768]{0:T(1024)S(1)} %copy-done.68, bf16[512,768]{1,0:T(8,128)(2,1)} %collective-permute-done.5, bf16[512,768]{1,0:T(8,128)(2,1)} %bitcast_multiply_fusion, f32[1024,1536]{1,0:T(8,128)} %copy-done.89, f32[1536]{0:T(1024)S(1)} %dynamic-slice_convert_fusion), kind=kOutput, calls=%fused_computation.11 | convolution fusion | flops 2437545984 | bytes 10232832 | tf_op jit(solution)/shard_map/dot_general | solution.py:203
  104.5 6.9 %fusion.10 = f32[1024,768]{1,0:T(8,128)} fusion(bf16[1024,1536]{1,0:T(8,128)(2,1)S(1)} %copy-done.88, bf16[768,3072]{1,0:T(8,128)(2,1)} %param.24, s32[]{:T(128)S(6)} %select_n.310), kind=kOutput, calls=%fused_computation.26 | convolution fusion | flops 2415919104 | bytes 8650756 | tf_op jit(solution)/shard_map/dot_general | solution.py:207
  111.4 4.3 %convolution_convert_fusion.1 = bf16[768,1536]{1,0:T(8,128)(2,1)S(1)} fusion(bf16[1024,1536]{1,0:T(8,128)(2,1)S(1)} %copy-done.88, bf16[512,768]{1,0:T(8,128)(2,1)} %collective-permute-done.3, bf16[512,768]{1,0:T(8,128)(2,1)} %add_convert_fusion.2), kind=kOutput, calls=%fused_computation.12 | convolution fusion | flops 2420244480 | bytes 7077888 | tf_op jit(solution)/shard_map/dot_general | solution.py:203
  121.8 7.5 %convert_reduce_fusion.1 = (f32[768]{0:T(1024)S(1)}, f32[768]{0:T(1024)}, f32[1024,768]{1,0:T(8,128)}) fusion(f32[768]{0:T(1024)S(1)} %copy-done.68, bf16[512,768]{1,0:T(8,128)(2,1)} %collective-permute-done.5, bf16[512,768]{1,0:T(8,128)(2,1)} %bitcast_multiply_fusion, bf16[3072,768]{1,0:T(8,128)(2,1)S(1)} %bitcast.253, s32[]{:T(128)S(6)} %select_n.310, ...), kind=kOutput, calls=%fused_computation.14 | convolution fusion | flops 2439510528 | bytes 13387780 | tf_op jit(solution)/shard_map/dot_general | solution.py:199
  142.0 2.8 multiply_reduce_fusion.2
  144.9 3.7 %multiply_reduce_fusion.3 = (f32[768]{0:T(1024)S(1)}, f32[512,768]{1,0:T(8,128)S(1)}, f32[768]{0:T(1024)S(1)}, bf16[1,512,768]{2,1,0:T(8,128)(2,1)}) fusion(f32[512,768]{1,0:T(8,128)S(1)} %copy-done.26, f32[512]{0:T(512)S(1)} %broadcast_multiply_fusion.3, f32[512,768]{1,0:T(8,128)S(1)} %copy-done.8, f32[512]{0:T(512)S(1)} %copy-done.57, ...), kind=kLoop, calls=%fused_computation.69 | loop fusion | flops 7862784 | bytes 11823104 | tf_op jit(solution)/shard_map/reduce_sum | solution.py:349
  150.4 3.5 %collective-permute-start.38 = (bf16[48,1536]{1,0:T(8,128)(2,1)S(1)}, bf16[48,1536]{1,0:T(8,128)(2,1)S(1)}, u32[]{:S(2)}, u32[]{:S(2)}) collective-permute-start(bf16[48,1536]{1,0:T(8,128)(2,1)S(1)} %get-tuple-element.90), channel_id=1, source_target_pairs={{0,16},{2,18},{4,20},{6,22},{8,24},{10,26},{12,28},{14,30},{16,0},... | collective-permute-start | bytes 442376 | tf_op jit(solution)/shard_map/ppermute | solution.py:241
  154.3 4.6 %collective-permute-done.37 = bf16[48,1536]{1,0:T(8,128)(2,1)S(1)} collective-permute-done((bf16[48,1536]{1,0:T(8,128)(2,1)S(1)}, bf16[48,1536]{1,0:T(8,128)(2,1)S(1)}, u32[]{:S(2)}, u32[]{:S(2)}) %collective-permute-start.37) | collective-permute-done | bytes 147488 | tf_op jit(solution)/shard_map/ppermute | solution.py:241
  158.9 4.2 %collective-permute-done.38 = bf16[48,1536]{1,0:T(8,128)(2,1)S(1)} collective-permute-done((bf16[48,1536]{1,0:T(8,128)(2,1)S(1)}, bf16[48,1536]{1,0:T(8,128)(2,1)S(1)}, u32[]{:S(2)}, u32[]{:S(2)}) %collective-permute-start.38) | collective-permute-done | bytes 147488 | tf_op jit(solution)/shard_map/ppermute | solution.py:241
  173.1 17.5 %shard_map.247 = (f32[384,1024]{1,0:T(8,128)}, f32[1024,384]{1,0:T(8,128)}, bf16[1024,384]{1,0:T(8,128)(2,1)S(1)}) custom-call(bf16[6,1024,1024]{2,1,0:T(8,128)(2,1)} %get-tuple-element.20.prob_ref, f32[3,8,1024]{2,1,0:T(8,128)S(1)} %copy-done.6, bf16[384,1024]{1,0:T(8,128)(2,1)S(1)} %convolution_convert_fusion.3.gt_ref, ...), custom_call_target="tpu_custom_call" | custom-call | flops 6442450944 | bytes 12582912 | tf_op jit(solution)/shard_map/pallas_call | solution.py:141
  200.5 4.0 %convolution_convert_fusion.2 = bf16[768,1152]{1,0:T(8,128)(2,1)S(1)} fusion(bf16[1024,768]{1,0:T(8,128)(2,1)} %copy-done.34, bf16[1024,384]{1,0:T(8,128)(2,1)S(1)} %copy-done.4, bf16[1024,384]{1,0:T(8,128)(2,1)} %get-tuple-element.55, bf16[1024,384]{1,0:T(8,128)(2,1)S(1)} %get-tuple-element.54), kind=kOutput, calls=%fused_computation.13 | convolution fusion | flops 1819901952 | bytes 5701632 | tf_op jit(solution)/shard_map/dot_general | solution.py:203
  204.6 3.5 %fusion.14 = f32[1024,768]{1,0:T(8,128)S(1)} fusion(bf16[768,384]{1,0:T(8,128)(2,1)S(1)} %copy-done.40, bf16[768,384]{1,0:T(8,128)(2,1)S(1)} %copy-done.44, bf16[768,384]{1,0:T(8,128)(2,1)S(1)} %copy-done.42, bf16[1024,384]{1,0:T(8,128)(2,1)S(1)} %copy-done.4, bf16[1024,384]{1,0:T(8,128)(2,1)S(1)} %copy-done.38, bf16[1024,384]{1,0:T(8,128)(2,1)} %copy-done.37), kind=kOutput, calls=%fused_computation.30 | convolution fusion | flops 1824325632 | bytes 7274496 | tf_op jit(solution)/shard_map/dot_general | solution.py:207
  217.2 10.2 %collective-permute-done.25 = bf16[4,2,48,192]{3,2,1,0:T(8,128)(2,1)S(1)} collective-permute-done((bf16[4,2,48,192]{3,2,1,0:T(8,128)(2,1)S(1)}, bf16[4,2,48,192]{3,2,1,0:T(8,128)(2,1)S(1)}, u32[]{:S(2)}, u32[]{:S(2)}) %collective-permute-start.25) | collective-permute-done | bytes 147488 | tf_op jit(solution)/shard_map/ppermute | solution.py:230
  228.0 8.6 %collective-permute-done.27 = bf16[4,2,48,192]{3,2,1,0:T(8,128)(2,1)S(1)} collective-permute-done((bf16[4,2,48,192]{3,2,1,0:T(8,128)(2,1)S(1)}, bf16[4,2,48,192]{3,2,1,0:T(8,128)(2,1)S(1)}, u32[]{:S(2)}, u32[]{:S(2)}) %collective-permute-start.27) | collective-permute-done | bytes 147488 | tf_op jit(solution)/shard_map/ppermute | solution.py:231
  243.5 5.6 %collective-permute-done.28 = bf16[4,48,192]{2,1,0:T(8,128)(2,1)S(1)} collective-permute-done((bf16[4,48,192]{2,1,0:T(8,128)(2,1)S(1)}, bf16[4,48,192]{2,1,0:T(8,128)(2,1)S(1)}, u32[]{:S(2)}, u32[]{:S(2)}) %collective-permute-start.28) | collective-permute-done | bytes 73760 | tf_op jit(solution)/shard_map/ppermute | solution.py:235
  249.2 3.6 %collective-permute-start.29 = (bf16[48,384]{1,0:T(8,128)(2,1)S(1)}, bf16[48,384]{1,0:T(8,128)(2,1)S(1)}, u32[]{:S(2)}, u32[]{:S(2)}) collective-permute-start(bf16[48,384]{1,0:T(8,128)(2,1)S(1)} %get-tuple-element.103), channel_id=1, source_target_pairs={{0,8},{2,10},{4,12},{6,14},{8,16},{10,18},{12,20},{14,22},{16,24},... | collective-permute-start | bytes 110600 | tf_op jit(solution)/shard_map/ppermute | solution.py:241
  259.1 2.8 collective-permute-start.47
  266.7 6.3 %collective-permute-start.21 = (bf16[48,1152]{1,0:T(8,128)(2,1)S(1)}, bf16[48,1152]{1,0:T(8,128)(2,1)S(1)}, u32[]{:S(2)}, u32[]{:S(2)}) collective-permute-start(bf16[48,1152]{1,0:T(8,128)(2,1)S(1)} %get-tuple-element.95), channel_id=1, source_target_pairs={{0,16},{2,18},{4,20},{6,22},{8,24},{10,26},{12,28},{14,30},{16,0},... | collective-permute-start | bytes 331784 | tf_op jit(solution)/shard_map/ppermute | solution.py:241
  273.0 5.5 %collective-permute-start.22 = (bf16[48,1152]{1,0:T(8,128)(2,1)S(1)}, bf16[48,1152]{1,0:T(8,128)(2,1)S(1)}, u32[]{:S(2)}, u32[]{:S(2)}) collective-permute-start(bf16[48,1152]{1,0:T(8,128)(2,1)S(1)} %get-tuple-element.96), channel_id=1, source_target_pairs={{0,24},{2,26},{4,28},{6,30},{8,0},{10,2},{12,4},{14,6},{16,8},{18,... | collective-permute-start | bytes 331784 | tf_op jit(solution)/shard_map/ppermute | solution.py:241
  279.3 3.6 %collective-permute-done.21 = bf16[48,1152]{1,0:T(8,128)(2,1)S(1)} collective-permute-done((bf16[48,1152]{1,0:T(8,128)(2,1)S(1)}, bf16[48,1152]{1,0:T(8,128)(2,1)S(1)}, u32[]{:S(2)}, u32[]{:S(2)}) %collective-permute-start.21) | collective-permute-done | bytes 110624 | tf_op jit(solution)/shard_map/ppermute | solution.py:241
  289.3 3.3 %fusion.39 = bf16[1,512,768]{2,1,0:T(8,128)(2,1)} fusion(f32[512,768]{1,0:T(8,128)S(1)} %copy-done.11, f32[1024,768]{1,0:T(8,128)} %get-tuple-element.65, f32[512]{0:T(512)} %broadcast_multiply_fusion.1, f32[512]{0:T(512)} %broadcast_multiply_fusion.2, f32[768]{0:T(1024)} %copy-done.52, f32[768]{0:T(1024)} %copy-done.48, f32[512]{0:T(512)} %slice.178, ...), kind=kLoop, calls=%fused_computation.100 | loop fusion | flops 3932160 | bytes 6303744 | tf_op jit(solution)/shard_map/broadcast_in_dim | solution.py:433
  301.7 2.8 collective-permute-start.13
  (456 shorter events, 138.0 us)
Async XLA Ops:
  0.7 10.7 %collective-permute-start.1 = (s32[512]{0:T(512)}, s32[512]{0:T(512)S(1)}, u32[]{:S(2)}, u32[]{:S(2)}) collective-permute-start(s32[512]{0:T(512)} %bitcast.248), channel_id=1, source_target_pairs={{0,1},{1,0},{2,3},{3,2},{4,5},{5,4},{6,7},{7,6},{8,9},{9,8},{10,11... | collective-permute-start | bytes 6152 | tf_op jit(solution)/shard_map/ppermute | solution.py:270
  4.1 71.0 %collective-permute-start.5 = (bf16[512,768]{1,0:T(8,128)(2,1)}, bf16[512,768]{1,0:T(8,128)(2,1)}, u32[]{:S(2)}, u32[]{:S(2)}) collective-permute-start(bf16[512,768]{1,0:T(8,128)(2,1)} %bitcast_multiply_fusion), channel_id=1, source_target_pairs={{0,1},{1,0},{2,3},{3,2},{4,5},{5,4},{6,7},{7,6},{8,9},{9,8},{10,11... | collective-permute-start | bytes 2359304 | tf_op jit(solution)/shard_map/ppermute | solution.py:270
  4.2 16.5 %collective-permute-start = (bf16[512,768]{1,0:T(8,128)(2,1)S(1)}, bf16[512,768]{1,0:T(8,128)(2,1)S(1)}, u32[]{:S(2)}, u32[]{:S(2)}) collective-permute-start(bf16[512,768]{1,0:T(8,128)(2,1)S(1)} %bitcast.221), channel_id=1, source_target_pairs={{0,1},{1,0},{2,3},{3,2},{4,5},{5,4},{6,7},{7,6},{8,9},{9,8},{10,11... | collective-permute-start | bytes 2359304 | tf_op jit(solution)/shard_map/ppermute | solution.py:270
  52.9 25.6 %collective-permute-start.3 = (bf16[512,768]{1,0:T(8,128)(2,1)}, bf16[512,768]{1,0:T(8,128)(2,1)}, u32[]{:S(2)}, u32[]{:S(2)}) collective-permute-start(bf16[512,768]{1,0:T(8,128)(2,1)} %add_convert_fusion.2), channel_id=1, source_target_pairs={{0,1},{1,0},{2,3},{3,2},{4,5},{5,4},{6,7},{7,6},{8,9},{9,8},{10,11... | collective-permute-start | bytes 2359304 | tf_op jit(solution)/shard_map/ppermute | solution.py:270
  95.3 39.4 %collective-permute-start.10 = (f32[1536]{0:T(1024)}, f32[1536]{0:T(1024)}, u32[]{:S(2)}, u32[]{:S(2)}) collective-permute-start(f32[1536]{0:T(1024)} %get-tuple-element.133), channel_id=1, source_target_pairs={{0,1},{1,0},{2,3},{3,2},{4,5},{5,4},{6,7},{7,6},{8,9},{9,8},{10,11... | collective-permute-start | bytes 18440 | tf_op jit(solution)/shard_map/ppermute | solution.py:270
  104.0 59.3 %collective-permute-start.41 = (bf16[1536,384]{1,0:T(8,128)(2,1)}, bf16[1536,384]{1,0:T(8,128)(2,1)}, u32[]{:S(2)}, u32[]{:S(2)}) collective-permute-start(bf16[1536,384]{1,0:T(8,128)(2,1)} %constant_dynamic-slice_fusion.6), channel_id=1, source_target_pairs={{0,1},{1,0},{2,3},{3,2},{4,5},{5,4},{6,7},{7,6},{8,9},{9,8},{10,11... | collective-permute-start | bytes 3538952 | tf_op jit(solution)/shard_map/ppermute | solution.py:270
  118.7 19.3 %collective-permute-start.33 = (bf16[4,2,48,768]{3,2,1,0:T(8,128)(2,1)}, bf16[4,2,48,768]{3,2,1,0:T(8,128)(2,1)}, u32[]{:S(2)}, u32[]{:S(2)}) collective-permute-start(bf16[4,2,48,768]{3,2,1,0:T(8,128)(2,1)} %dynamic-slice_bitcast_fusion.3), channel_id=1, source_target_pairs={{0,2},{2,0},{4,6},{6,4},{8,10},{10,8},{12,14},{14,12},{16,18},{18,... | collective-permute-start | bytes 1769480 | tf_op jit(solution)/shard_map/ppermute | solution.py:230
  120.2 19.8 %collective-permute-start.35 = (bf16[4,2,48,768]{3,2,1,0:T(8,128)(2,1)}, bf16[4,2,48,768]{3,2,1,0:T(8,128)(2,1)}, u32[]{:S(2)}, u32[]{:S(2)}) collective-permute-start(bf16[4,2,48,768]{3,2,1,0:T(8,128)(2,1)} %dynamic-slice_bitcast_fusion.2), channel_id=1, source_target_pairs={{0,4},{2,6},{4,0},{6,2},{8,12},{10,14},{12,8},{14,10},{16,20},{18,... | collective-permute-start | bytes 1769480 | tf_op jit(solution)/shard_map/ppermute | solution.py:231
  134.7 10.1 %collective-permute-start.4 = (bf16[512,768]{1,0:T(8,128)(2,1)}, bf16[512,768]{1,0:T(8,128)(2,1)}, u32[]{:S(2)}, u32[]{:S(2)}) collective-permute-start(bf16[512,768]{1,0:T(8,128)(2,1)} %slice.311), channel_id=1, source_target_pairs={{0,1},{1,0},{2,3},{3,2},{4,5},{5,4},{6,7},{7,6},{8,9},{9,8},{10,11... | collective-permute-start | bytes 2359304 | tf_op jit(solution)/shard_map/ppermute | solution.py:270
  139.5 9.9 %collective-permute-start.34 = (bf16[4,48,768]{2,1,0:T(8,128)(2,1)S(1)}, bf16[4,48,768]{2,1,0:T(8,128)(2,1)S(1)}, u32[]{:S(2)}, u32[]{:S(2)}) collective-permute-start(bf16[4,48,768]{2,1,0:T(8,128)(2,1)S(1)} %dynamic-slice_bitcast_fusion.9), channel_id=1, source_target_pairs={{0,4},{2,6},{4,0},{6,2},{8,12},{10,14},{12,8},{14,10},{16,20},{18,... | collective-permute-start | bytes 884744 | tf_op jit(solution)/shard_map/ppermute | solution.py:234
  141.4 8.7 %collective-permute-start.36 = (bf16[4,48,768]{2,1,0:T(8,128)(2,1)S(1)}, bf16[4,48,768]{2,1,0:T(8,128)(2,1)S(1)}, u32[]{:S(2)}, u32[]{:S(2)}) collective-permute-start(bf16[4,48,768]{2,1,0:T(8,128)(2,1)S(1)} %dynamic-slice_bitcast_fusion.8), channel_id=1, source_target_pairs={{0,2},{2,0},{4,6},{6,4},{8,10},{10,8},{12,14},{14,12},{16,18},{18,... | collective-permute-start | bytes 884744 | tf_op jit(solution)/shard_map/ppermute | solution.py:235
  150.4 12.6 %collective-permute-start.38 = (bf16[48,1536]{1,0:T(8,128)(2,1)S(1)}, bf16[48,1536]{1,0:T(8,128)(2,1)S(1)}, u32[]{:S(2)}, u32[]{:S(2)}) collective-permute-start(bf16[48,1536]{1,0:T(8,128)(2,1)S(1)} %get-tuple-element.90), channel_id=1, source_target_pairs={{0,16},{2,18},{4,20},{6,22},{8,24},{10,26},{12,28},{14,30},{16,0},... | collective-permute-start | bytes 442376 | tf_op jit(solution)/shard_map/ppermute | solution.py:241
  153.9 9.2 %collective-permute-start.39 = (bf16[48,1536]{1,0:T(8,128)(2,1)S(1)}, bf16[48,1536]{1,0:T(8,128)(2,1)S(1)}, u32[]{:S(2)}, u32[]{:S(2)}) collective-permute-start(bf16[48,1536]{1,0:T(8,128)(2,1)S(1)} %get-tuple-element.91), channel_id=1, source_target_pairs={{0,24},{2,26},{4,28},{6,30},{8,0},{10,2},{12,4},{14,6},{16,8},{18,... | collective-permute-start | bytes 442376 | tf_op jit(solution)/shard_map/ppermute | solution.py:241
  154.2 17.5 %collective-permute-start.7 = (bf16[512,768]{1,0:T(8,128)(2,1)S(1)}, bf16[512,768]{1,0:T(8,128)(2,1)S(1)}, u32[]{:S(2)}, u32[]{:S(2)}) collective-permute-start(bf16[512,768]{1,0:T(8,128)(2,1)S(1)} %multiply_convert_fusion.2), channel_id=1, source_target_pairs={{0,1},{1,0},{2,3},{3,2},{4,5},{5,4},{6,7},{7,6},{8,9},{9,8},{10,11... | collective-permute-start | bytes 2359304 | tf_op jit(solution)/shard_map/ppermute | solution.py:270
  167.1 44.1 %collective-permute-start.42 = (bf16[4,2,192,192]{3,2,1,0:T(8,128)(2,1)}, bf16[4,2,192,192]{3,2,1,0:T(8,128)(2,1)}, u32[]{:S(2)}, u32[]{:S(2)}) collective-permute-start(bf16[4,2,192,192]{3,2,1,0:T(8,128)(2,1)} %dynamic-slice_bitcast_fusion.1), channel_id=1, source_target_pairs={{0,2},{2,0},{4,6},{6,4},{8,10},{10,8},{12,14},{14,12},{16,18},{18,... | collective-permute-start | bytes 1769480 | tf_op jit(solution)/shard_map/ppermute | solution.py:230
  169.3 43.4 %collective-permute-start.44 = (bf16[4,2,192,192]{3,2,1,0:T(8,128)(2,1)}, bf16[4,2,192,192]{3,2,1,0:T(8,128)(2,1)}, u32[]{:S(2)}, u32[]{:S(2)}) collective-permute-start(bf16[4,2,192,192]{3,2,1,0:T(8,128)(2,1)} %dynamic-slice_bitcast_fusion), channel_id=1, source_target_pairs={{0,4},{2,6},{4,0},{6,2},{8,12},{10,14},{12,8},{14,10},{16,20},{18,... | collective-permute-start | bytes 1769480 | tf_op jit(solution)/shard_map/ppermute | solution.py:231
  209.5 28.3 %collective-permute-start.16 = (bf16[4,2,48,576]{3,2,1,0:T(8,128)(2,1)S(1)}, bf16[4,2,48,576]{3,2,1,0:T(8,128)(2,1)S(1)}, u32[]{:S(2)}, u32[]{:S(2)}) collective-permute-start(bf16[4,2,48,576]{3,2,1,0:T(8,128)(2,1)S(1)} %dynamic-slice_bitcast_fusion.5), channel_id=1, source_target_pairs={{0,2},{2,0},{4,6},{6,4},{8,10},{10,8},{12,14},{14,12},{16,18},{18,... | collective-permute-start | bytes 1327112 | tf_op jit(solution)/shard_map/ppermute | solution.py:230
  210.5 28.0 %collective-permute-start.18 = (bf16[4,2,48,576]{3,2,1,0:T(8,128)(2,1)S(1)}, bf16[4,2,48,576]{3,2,1,0:T(8,128)(2,1)S(1)}, u32[]{:S(2)}, u32[]{:S(2)}) collective-permute-start(bf16[4,2,48,576]{3,2,1,0:T(8,128)(2,1)S(1)} %dynamic-slice_bitcast_fusion.4), channel_id=1, source_target_pairs={{0,4},{2,6},{4,0},{6,2},{8,12},{10,14},{12,8},{14,10},{16,20},{18,... | collective-permute-start | bytes 1327112 | tf_op jit(solution)/shard_map/ppermute | solution.py:231
  211.2 72.4 %collective-permute-start.8 = (bf16[512,768]{1,0:T(8,128)(2,1)S(1)}, bf16[512,768]{1,0:T(8,128)(2,1)S(1)}, u32[]{:S(2)}, u32[]{:S(2)}) collective-permute-start(bf16[512,768]{1,0:T(8,128)(2,1)S(1)} %slice.309), channel_id=1, source_target_pairs={{0,1},{1,0},{2,3},{3,2},{4,5},{5,4},{6,7},{7,6},{8,9},{9,8},{10,11... | collective-permute-start | bytes 2359304 | tf_op jit(solution)/shard_map/ppermute | solution.py:270
  212.7 26.9 %collective-permute-start.43 = (bf16[4,192,192]{2,1,0:T(8,128)(2,1)S(1)}, bf16[4,192,192]{2,1,0:T(8,128)(2,1)S(1)}, u32[]{:S(2)}, u32[]{:S(2)}) collective-permute-start(bf16[4,192,192]{2,1,0:T(8,128)(2,1)S(1)} %dynamic-slice_bitcast_fusion.7), channel_id=1, source_target_pairs={{0,4},{2,6},{4,0},{6,2},{8,12},{10,14},{12,8},{14,10},{16,20},{18,... | collective-permute-start | bytes 884744 | tf_op jit(solution)/shard_map/ppermute | solution.py:234
  215.9 11.5 %collective-permute-start.25 = (bf16[4,2,48,192]{3,2,1,0:T(8,128)(2,1)S(1)}, bf16[4,2,48,192]{3,2,1,0:T(8,128)(2,1)S(1)}, u32[]{:S(2)}, u32[]{:S(2)}) collective-permute-start(bf16[4,2,48,192]{3,2,1,0:T(8,128)(2,1)S(1)} %dynamic-slice_bitcast_fusion.13), channel_id=1, source_target_pairs={{0,2},{2,0},{4,6},{6,4},{8,10},{10,8},{12,14},{14,12},{16,18},{18,... | collective-permute-start | bytes 442376 | tf_op jit(solution)/shard_map/ppermute | solution.py:230
  227.4 9.1 %collective-permute-start.27 = (bf16[4,2,48,192]{3,2,1,0:T(8,128)(2,1)S(1)}, bf16[4,2,48,192]{3,2,1,0:T(8,128)(2,1)S(1)}, u32[]{:S(2)}, u32[]{:S(2)}) collective-permute-start(bf16[4,2,48,192]{3,2,1,0:T(8,128)(2,1)S(1)} %dynamic-slice_bitcast_fusion.12), channel_id=1, source_target_pairs={{0,4},{2,6},{4,0},{6,2},{8,12},{10,14},{12,8},{14,10},{16,20},{18,... | collective-permute-start | bytes 442376 | tf_op jit(solution)/shard_map/ppermute | solution.py:231
  236.5 16.9 %collective-permute-start.45 = (bf16[4,192,192]{2,1,0:T(8,128)(2,1)S(1)}, bf16[4,192,192]{2,1,0:T(8,128)(2,1)S(1)}, u32[]{:S(2)}, u32[]{:S(2)}) collective-permute-start(bf16[4,192,192]{2,1,0:T(8,128)(2,1)S(1)} %dynamic-slice_bitcast_fusion.6), channel_id=1, source_target_pairs={{0,2},{2,0},{4,6},{6,4},{8,10},{10,8},{12,14},{14,12},{16,18},{18,... | collective-permute-start | bytes 884744 | tf_op jit(solution)/shard_map/ppermute | solution.py:235
  238.4 10.6 %collective-permute-start.28 = (bf16[4,48,192]{2,1,0:T(8,128)(2,1)S(1)}, bf16[4,48,192]{2,1,0:T(8,128)(2,1)S(1)}, u32[]{:S(2)}, u32[]{:S(2)}) collective-permute-start(bf16[4,48,192]{2,1,0:T(8,128)(2,1)S(1)} %dynamic-slice_bitcast_fusion.14), channel_id=1, source_target_pairs={{0,2},{2,0},{4,6},{6,4},{8,10},{10,8},{12,14},{14,12},{16,18},{18,... | collective-permute-start | bytes 221192 | tf_op jit(solution)/shard_map/ppermute | solution.py:235
  239.5 23.1 %collective-permute-start.17 = (bf16[4,48,576]{2,1,0:T(8,128)(2,1)S(1)}, bf16[4,48,576]{2,1,0:T(8,128)(2,1)S(1)}, u32[]{:S(2)}, u32[]{:S(2)}) collective-permute-start(bf16[4,48,576]{2,1,0:T(8,128)(2,1)S(1)} %dynamic-slice_bitcast_fusion.11), channel_id=1, source_target_pairs={{0,4},{2,6},{4,0},{6,2},{8,12},{10,14},{12,8},{14,10},{16,20},{18,... | collective-permute-start | bytes 663560 | tf_op jit(solution)/shard_map/ppermute | solution.py:234
  259.1 13.9 %collective-permute-start.47 = (bf16[192,384]{1,0:T(8,128)(2,1)S(1)}, bf16[192,384]{1,0:T(8,128)(2,1)S(1)}, u32[]{:S(2)}, u32[]{:S(2)}) collective-permute-start(bf16[192,384]{1,0:T(8,128)(2,1)S(1)} %get-tuple-element.87), channel_id=1, source_target_pairs={{0,16},{2,18},{4,20},{6,22},{8,24},{10,26},{12,28},{14,30},{16,0},... | collective-permute-start | bytes 442376 | tf_op jit(solution)/shard_map/ppermute | solution.py:241
  262.6 15.9 %collective-permute-start.48 = (bf16[192,384]{1,0:T(8,128)(2,1)S(1)}, bf16[192,384]{1,0:T(8,128)(2,1)S(1)}, u32[]{:S(2)}, u32[]{:S(2)}) collective-permute-start(bf16[192,384]{1,0:T(8,128)(2,1)S(1)} %get-tuple-element.88), channel_id=1, source_target_pairs={{0,24},{2,26},{4,28},{6,30},{8,0},{10,2},{12,4},{14,6},{16,8},{18,... | collective-permute-start | bytes 442376 | tf_op jit(solution)/shard_map/ppermute | solution.py:241
  264.0 15.4 %collective-permute-start.20 = (bf16[48,1152]{1,0:T(8,128)(2,1)S(1)}, bf16[48,1152]{1,0:T(8,128)(2,1)S(1)}, u32[]{:S(2)}, u32[]{:S(2)}) collective-permute-start(bf16[48,1152]{1,0:T(8,128)(2,1)S(1)} %get-tuple-element.94), channel_id=1, source_target_pairs={{0,8},{2,10},{4,12},{6,14},{8,16},{10,18},{12,20},{14,22},{16,24},... | collective-permute-start | bytes 331784 | tf_op jit(solution)/shard_map/ppermute | solution.py:241
  266.7 16.2 %collective-permute-start.21 = (bf16[48,1152]{1,0:T(8,128)(2,1)S(1)}, bf16[48,1152]{1,0:T(8,128)(2,1)S(1)}, u32[]{:S(2)}, u32[]{:S(2)}) collective-permute-start(bf16[48,1152]{1,0:T(8,128)(2,1)S(1)} %get-tuple-element.95), channel_id=1, source_target_pairs={{0,16},{2,18},{4,20},{6,22},{8,24},{10,26},{12,28},{14,30},{16,0},... | collective-permute-start | bytes 331784 | tf_op jit(solution)/shard_map/ppermute | solution.py:241
  273.0 9.9 %collective-permute-start.22 = (bf16[48,1152]{1,0:T(8,128)(2,1)S(1)}, bf16[48,1152]{1,0:T(8,128)(2,1)S(1)}, u32[]{:S(2)}, u32[]{:S(2)}) collective-permute-start(bf16[48,1152]{1,0:T(8,128)(2,1)S(1)} %get-tuple-element.96), channel_id=1, source_target_pairs={{0,24},{2,26},{4,28},{6,30},{8,0},{10,2},{12,4},{14,6},{16,8},{18,... | collective-permute-start | bytes 331784 | tf_op jit(solution)/shard_map/ppermute | solution.py:241
  279.3 15.6 %collective-permute-start.49 = (bf16[192,384]{1,0:T(8,128)(2,1)}, bf16[192,384]{1,0:T(8,128)(2,1)}, u32[]{:S(2)}, u32[]{:S(2)}) collective-permute-start(bf16[192,384]{1,0:T(8,128)(2,1)} %fusion.48), channel_id=1, source_target_pairs={{0,1},{1,0},{2,3},{3,2},{4,5},{5,4},{6,7},{7,6},{8,9},{9,8},{10,11... | collective-permute-start | bytes 442376 | tf_op jit(solution)/shard_map/ppermute | solution.py:270
  283.6 28.6 %collective-permute-start.23 = (bf16[48,1152]{1,0:T(8,128)(2,1)}, bf16[48,1152]{1,0:T(8,128)(2,1)}, u32[]{:S(2)}, u32[]{:S(2)}) collective-permute-start(bf16[48,1152]{1,0:T(8,128)(2,1)} %fusion.54), channel_id=1, source_target_pairs={{0,1},{1,0},{2,3},{3,2},{4,5},{5,4},{6,7},{7,6},{8,9},{9,8},{10,11... | collective-permute-start | bytes 331784 | tf_op jit(solution)/shard_map/ppermute | solution.py:270
  (119 other events, 850.7 us)

commit v2 on v0

--- a/solution.py
+++ b/solution.py
@@ -1,15 +1,1003 @@
+import functools
+
 import jax
 import jax.numpy as jnp
+import numpy as np
 from jax import lax
+from jax.experimental import pallas as pl
+from jax.experimental.pallas import tpu as pltpu
 from jax.sharding import PartitionSpec as P
 
 HEADS = 12
 HEAD_DIM = 64
-
-
 EPS = 1e-05
 SCORE_SCALE = 0.125
 NEG_START = -1e30
+F32, BF16 = jnp.float32, jnp.bfloat16
+COST = 2e8
+
+
+def dot(a, b):
+    return jnp.dot(a, b, preferred_element_type=F32)
+
+
+def dot_tn(a, b):
+    return lax.dot_general(a, b, (((0,), (0,)), ((), ())), preferred_element_type=F32)
+
+
+def dot_nt(a, b):
+    return lax.dot_general(a, b, (((1,), (1,)), ((), ())), preferred_element_type=F32)
+
+
+def sds(shape, dtype):
+    return jax.ShapeDtypeStruct(shape, dtype)
+
+
+def hbm(x):
+    return pltpu.with_memory_space_constraint(x, pltpu.HBM)
+
+
+class Order:
+    def __init__(self, place):
+        self.place, self.token = place, None
+
+    def call(
+        self, body, args, grid, in_specs, out_specs, out_shape, scratch=(), mb=32, us=1.0, aliases=None, after=(),
+        name=None,
+    ):
+        after = list(after) + ([] if self.token is None else [self.token])
+        extra, n_in, n_out = len(after), 1 + len(args), len(out_shape)
+
+        def inner(*refs):
+            outs = refs[n_in + extra :]
+            body(*refs[:n_in], *outs[:n_out], *outs[n_out + 1 :])
+
+        *outs, self.token = pl.pallas_call(
+            inner,
+            grid_spec=pltpu.PrefetchScalarGridSpec(
+                num_scalar_prefetch=1,
+                grid=grid,
+                in_specs=list(in_specs) + [ANY] * extra,
+                out_specs=list(out_specs) + [ANY],
+                scratch_shapes=list(scratch),
+            ),
+            out_shape=list(out_shape) + [sds((8, 128), F32)],
+            input_output_aliases=aliases or {},
+            compiler_params=pltpu.CompilerParams(vmem_limit_bytes=mb << 20),
+            cost_estimate=pl.CostEstimate(flops=int(us * COST), bytes_accessed=1 << 16, transcendentals=0),
+            name=name,
+        )(self.place, *args, *after)
+        return outs
+
+
+ANY = pl.BlockSpec(memory_space=pl.ANY)
+
+
+def whole(shape):
+    return pl.BlockSpec(shape, lambda *a: (0,) * len(shape))
+
+
+def layer_stats(stream):
+    row_mean = jnp.mean(stream, axis=-1, keepdims=True)
+    centred = stream - row_mean
+    variance = jnp.mean(centred * centred, axis=-1, keepdims=True)
+    inv = lax.rsqrt(variance + EPS)
+    return centred * inv, inv
+
+
+def swap_lanes(x):
+    lane = lax.broadcasted_iota(jnp.int32, x.shape, 1) % HEAD_DIM
+    half = HEAD_DIM // 2
+    return jnp.where(lane < half, pltpu.roll(x, 128 - half, 1), pltpu.roll(x, half, 1))
+
+
+def mask_half(value, head):
+    lane = lax.broadcasted_iota(jnp.int32, value.shape, 1)
+    keep = (lane < HEAD_DIM) if head == 0 else (lane >= HEAD_DIM)
+    return jnp.where(keep, value, jnp.zeros_like(value))
+
+
+def attend_body(
+    s_ref, ta_ref, tb_ref, cond_ref, ada_ref, adab_ref, gain_ref, wq_ref, wk_ref, wv_ref, pa_ref, pb_ref, freq_ref,
+    cot_ref, abs_ref,
+    n1_out, q_out, k_out, v_out, cost_ref, sint_ref,
+    out_ref, prob_ref, inv_ref, mod_ref, wtd_ref, km_ref, vt_ref, n1_ref, q_ref, k_ref, v_ref,
+):
+    pair, step = pl.program_id(0), pl.program_id(1)
+    span, width = ta_ref.shape
+    blk = out_ref.shape[1]
+
+    @pl.when((pair == 0) & (step == 0))
+    def _():
+        kept = jnp.broadcast_to(abs_ref[...].astype(F32), (128, span)).T[:, 0:1]
+        wtd_ref[...] = (cot_ref[...].astype(F32) * kept).astype(BF16)
+        cond = jnp.broadcast_to(cond_ref[...].astype(F32), (16, cond_ref.shape[1])).astype(BF16)
+        mod_ref[...] = dot(cond, ada_ref[...])[:8] + adab_ref[...].astype(F32)[None, :]
+        shift, scale = mod_ref[0:1, 0:width], mod_ref[0:1, width : 2 * width]
+        gain = gain_ref[...].astype(F32)[None, :] * (1.0 + scale)
+        for half, (t_ref, p_ref) in enumerate(((ta_ref, pa_ref), (tb_ref, pb_ref))):
+            rows = slice(half * span, (half + 1) * span)
+            angles = freq_ref[...] * p_ref[...].astype(F32)
+            cos_h, sin_h = jnp.cos(angles), jnp.sin(angles)
+            cos_t, sin_t = rotation(cos_h, sin_h)
+            cost_ref[:, rows] = cos_h
+            sint_ref[:, rows] = sin_h
+            cos_n, sin_n = cos_t.T, sin_t.T
+            a_one, _ = layer_stats(t_ref[...].astype(F32))
+            normed = (a_one * gain + shift).astype(BF16)
+            n1_ref[rows, :] = normed
+            q_pre = dot(normed, wq_ref[...])
+            k_pre = dot(normed, wk_ref[...])
+            v_ref[rows, :] = dot(normed, wv_ref[...]).astype(BF16)
+            for p in range(q_pre.shape[1] // 128):
+                at = slice(p * 128, (p + 1) * 128)
+                part = q_pre[:, at]
+                q_ref[rows, at] = (SCORE_SCALE * (part * cos_n + swap_lanes(part) * sin_n)).astype(BF16)
+                part = k_pre[:, at]
+                k_ref[rows, at] = (part * cos_n + swap_lanes(part) * sin_n).astype(BF16)
+
+    lanes = pl.ds(pl.multiple_of(pair * 128, 128), 128)
+    piece = jnp.minimum(pair * pl.num_programs(1) + step, n1_ref.shape[0] // n1_out.shape[0] - 1)
+    n1_out[...] = n1_ref[pl.ds(pl.multiple_of(piece * n1_out.shape[0], 128), n1_out.shape[0]), :]
+
+    @pl.when(step == 0)
+    def _():
+        keys = k_ref[:, lanes]
+        q_out[...] = q_ref[:, lanes]
+        k_out[...] = keys
+        v_out[...] = v_ref[:, lanes]
+        for head in (0, 1):
+            km_ref[head] = mask_half(keys, head)
+        vt_ref[...] = v_ref[:, lanes].T
+
+    queries = q_ref[pl.ds(pl.multiple_of(step * blk, blk), blk), lanes]
+    for head in (0, 1):
+        rows = slice(head * HEAD_DIM, (head + 1) * HEAD_DIM)
+        scores = dot_nt(km_ref[head], queries)
+        top = jnp.max(scores, axis=0, keepdims=True)
+        raised = jnp.exp(scores - top)
+        total = jnp.sum(raised, axis=0, keepdims=True)
+        prob = raised.astype(BF16)
+        prob_ref[head] = prob
+        inverse = 1.0 / total
+        inv_ref[0, head : head + 1, :] = inverse
+        out_ref[rows, :] = (dot(vt_ref[rows, :], prob) * inverse).astype(BF16)
+
+
+def attend_call(order, tok, tok_o, cond, ada, adab, gain, qkv_weight, pos, pos_o, cot, absorbed):
+    span, width = tok.shape
+    length, hw = 2 * span, width // 2
+    pairs, blk = hw // 128, 512
+    freq = np.power(10000.0, -np.arange(0, HEAD_DIM, 2) / HEAD_DIM).astype(np.float32)[:, None]
+    wspec = lambda j: pl.BlockSpec((width, hw), lambda p, i, s: (0, 2 * j + s[0]))
+    col = pl.BlockSpec((length, 128), lambda p, i, s: (0, p))
+    return order.call(
+        attend_body,
+        [hbm(tok), tok_o, hbm(cond), hbm(ada), hbm(adab), hbm(gain), *[hbm(qkv_weight)] * 3, hbm(pos), pos_o, hbm(jnp.asarray(freq)), hbm(cot), hbm(absorbed)],
+        (pairs, length // blk),
+        [whole(tok.shape), whole(tok.shape), whole(cond.shape), whole(ada.shape), whole(adab.shape), whole(gain.shape), wspec(0), wspec(1), wspec(2),
+         whole(pos.shape), whole(pos.shape), whole(freq.shape), whole(cot.shape), whole(absorbed.shape)],
+        [pl.BlockSpec((length // 4, width), lambda p, i, s: (jnp.minimum(p * (length // blk) + i, 3), 0)),
+         col, col, col, whole((HEAD_DIM // 2, length)), whole((HEAD_DIM // 2, length)),
+         pl.BlockSpec((128, blk), lambda p, i, s: (p, i)),
+         pl.BlockSpec((2, length, blk), lambda p, i, s: (p, 0, i)),
+         pl.BlockSpec((1, 8, blk), lambda p, i, s: (p, 0, i)), whole((8, ada.shape[1])), whole(tok.shape)],
+        [sds((length, width), BF16)] + [sds((length, hw), BF16)] * 3
+        + [sds((HEAD_DIM // 2, length), F32)] * 2
+        + [sds((hw, length), BF16), pltpu.HBM((2 * pairs, length, length), BF16), sds((pairs, 8, length), F32),
+           sds((8, ada.shape[1]), F32), sds(tok.shape, BF16)],
+        scratch=[pltpu.VMEM((2, length, 128), BF16), pltpu.VMEM((128, length), BF16),
+                 pltpu.VMEM((length, width), BF16)] + [pltpu.VMEM((length, hw), BF16)] * 3,
+        mb=32, us=20, name="attend",
+    )
+
+
+def swap_rows(x):
+    half = HEAD_DIM // 2
+    return jnp.concatenate([x[half * j : half * (j + 1)] for j in (1, 0, 3, 2)], axis=0)
+
+
+def rotation(cos_h, sin_h):
+    return jnp.concatenate([cos_h] * 4, axis=0), jnp.concatenate([-sin_h, sin_h, -sin_h, sin_h], axis=0)
+
+
+def attn_bwd_body(
+    r, s_ref, prob_ref, inv_ref, gt_ref, out_ref, q_ref, k_ref, v_ref, cost_ref, sint_ref, n1_ref,
+    g_ref, keep_ref, send_ref, vm_ref, kt_ref, dk_acc, dv_acc, acc_ref,
+):
+    step = pl.program_id(1)
+    blk = q_ref.shape[0]
+
+    @pl.when(step == 0)
+    def _():
+        values = v_ref[...]
+        for head in (0, 1):
+            vm_ref[head] = mask_half(values, head)
+        kt_ref[...] = k_ref[...].T
+
+    queries = q_ref[...]
+    grad_t = gt_ref[...].astype(jnp.float32)
+    row_id = lax.broadcasted_iota(jnp.int32, (128, blk), 0)
+    inverse = jnp.where(row_id < HEAD_DIM, inv_ref[0, 0:1, :], inv_ref[0, 1:2, :])
+    grad_t = grad_t * inverse
+    product = grad_t * out_ref[...].astype(jnp.float32)
+    grad_b = grad_t.astype(jnp.bfloat16)
+    dk_new = None
+    dq_parts = []
+    for head in (0, 1):
+        rows = slice(head * HEAD_DIM, (head + 1) * HEAD_DIM)
+        delta = jnp.sum(product[rows], axis=0, keepdims=True)
+        keep = (row_id < HEAD_DIM) if head == 0 else (row_id >= HEAD_DIM)
+        grad_m = jnp.where(keep, grad_b, jnp.zeros_like(grad_b))
+        grad_p = jnp.dot(vm_ref[head], grad_b, preferred_element_type=jnp.float32)
+        prob = prob_ref[head]
+        grad_s = (prob.astype(jnp.float32) * (grad_p - delta)).astype(jnp.bfloat16)
+        dv_h = dot_nt(prob, grad_m)
+        dk_h = dot(grad_s, mask_half(queries, head))
+        if dk_new is None:
+            dk_new, dv_new = dk_h, dv_h
+        else:
+            dk_new, dv_new = dk_new + dk_h, dv_new + dv_h
+        dq_parts.append(dot(kt_ref[rows, :], grad_s) * SCORE_SCALE)
+    dq_t = jnp.concatenate(dq_parts, axis=0)
+    here = pl.ds(pl.multiple_of(step * blk, blk), blk)
+    cos_t, sin_t = rotation(cost_ref[:, here], sint_ref[:, here])
+    dq_t = dq_t * cos_t - swap_rows(dq_t) * sin_t
+    g_ref[here, 0:128] = dq_t.T.astype(jnp.bfloat16)
+
+    @pl.when(step == 0)
+    def _():
+        dk_acc[...] = dk_new
+        dv_acc[...] = dv_new
+
+    @pl.when(step > 0)
+    def _():
+        dk_acc[...] += dk_new
+        dv_acc[...] += dv_new
+
+    @pl.when(step == pl.num_programs(1) - 1)
+    def _():
+        dk = dk_acc[...]
+        cos_t, sin_t = rotation(cost_ref[...], sint_ref[...])
+        g_ref[:, 128:256] = (dk * cos_t.T - swap_lanes(dk) * sin_t.T).astype(jnp.bfloat16)
+        g_ref[:, 256:384] = dv_acc[...].astype(jnp.bfloat16)
+        acc_ref[...] = dot_tn(n1_ref[...], g_ref[...]).astype(jnp.bfloat16)
+        store_parts(s_ref, acc_ref, r, keep_ref, send_ref)
+
+
+def attn_bwd(
+    order, start, count, prob, inverse, grad_t, out_t, queries, keys, values, cos_t, sin_t, normed_one,
+    old, block, blocks,
+):
+    length = keys.shape[0]
+    width = normed_one.shape[1]
+    blk = 512
+    r = width // 16
+    col = pl.BlockSpec((length, 128), lambda p, i, s: (0, p + start))
+    rowt = pl.BlockSpec((128, blk), lambda p, i, s: (p + start, i))
+    out = pl.BlockSpec((2, 4, r, 384), lambda p, i, s: (0, 0, 0, p + block))
+    args = [prob, inverse, grad_t, out_t, queries, keys, values, cos_t, sin_t, normed_one]
+    aliases = {}
+    after = []
+    if old is not None:
+        aliases = {1 + len(args) + j: 1 + j for j in range(2)}
+        after = list(old)
+    return order.call(
+        functools.partial(attn_bwd_body, r), args, (count, length // blk),
+        [
+            pl.BlockSpec((2, length, blk), lambda p, i, s: (p + start, 0, i)),
+            pl.BlockSpec((1, 8, blk), lambda p, i, s: (p + start, 0, i)),
+            rowt, rowt,
+            pl.BlockSpec((blk, 128), lambda p, i, s: (i, p + start)),
+            col, col, whole(cos_t.shape), whole(cos_t.shape), whole(normed_one.shape),
+        ],
+        [pl.BlockSpec((length, 384), lambda p, i, s: (0, p))] + [out] * 2,
+        [sds((length, 384 * count), BF16)] + [sds((2, 4, r, 384 * blocks), BF16)] * 2,
+        scratch=[
+            pltpu.VMEM((2, length, 128), BF16),
+            pltpu.VMEM((128, length), BF16),
+            pltpu.VMEM((length, 128), F32),
+            pltpu.VMEM((length, 128), F32),
+            pltpu.VMEM((width, 384), BF16),
+        ],
+        mb=18, us=8.0 * count, aliases=aliases, after=after, name="attn_bwd",
+    )
+
+
+def mix_body(s_ref, own_ref, got_ref, mid_ref, wtd_ref, mod_ref, bias_ref, out_ref, sum_ref):
+    width = mid_ref.shape[1]
+    branch = own_ref[...] + got_ref[...].astype(F32) + bias_ref[...].astype(F32)[None, :]
+    out_ref[...] = (mid_ref[...] + mod_ref[0:1, 5 * width : 6 * width] * branch).astype(BF16)
+
+    @pl.when(pl.program_id(0) == 0)
+    def _():
+        sum_ref[...] = jnp.zeros_like(sum_ref)
+
+    sum_ref[0:1, :] += jnp.sum(wtd_ref[...].astype(F32) * branch, axis=0, keepdims=True)
+
+
+def mix_call(order, own, got, mid, wtd, mod, bias):
+    span, width = mid.shape
+    blk = 256
+    row = pl.BlockSpec((blk, width), lambda i, s: (i, 0))
+    return order.call(
+        mix_body, [own, got, mid, wtd, mod, bias], (span // blk,),
+        [row] * 4 + [whole(mod.shape), whole(bias.shape)],
+        [row, whole((8, width))], [sds((span, width), BF16), sds((8, width), F32)],
+        mb=8, us=2.5, name="mix",
+    )
+
+
+def post_body(s_ref, att_ref, oth_ref, wm_ref, wo_ref, tok_ref, mod_ref, gain_ref, mid_ref, br_ref, n2_ref):
+    width = tok_ref.shape[1]
+    branch = dot_tn(att_ref[...], wm_ref[...]) + dot_tn(oth_ref[...], wo_ref[...])
+    br_ref[...] = branch
+    middle = tok_ref[...].astype(F32) + mod_ref[0:1, 2 * width : 3 * width] * branch
+    mid_ref[...] = middle
+    a_two, _ = layer_stats(middle)
+    scale = mod_ref[0:1, 4 * width : 5 * width]
+    n2_ref[...] = (
+        a_two * (gain_ref[...].astype(F32)[None, :] * (1.0 + scale)) + mod_ref[0:1, 3 * width : 4 * width]
+    ).astype(BF16)
+
+
+def post_call(order, att_t, att_o, out_weight, tok, mod, gain):
+    span, width = tok.shape
+    hw = width // 2
+    blk = 256
+    n = span // blk
+    row = pl.BlockSpec((blk, width), lambda i, s: (i, 0))
+    return order.call(
+        post_body, [att_t, att_o, out_weight, out_weight, tok, mod, gain], (n,),
+        [
+            pl.BlockSpec((hw, blk), lambda i, s: (0, i)),
+            pl.BlockSpec((hw, blk), lambda i, s: (0, i + n)),
+            pl.BlockSpec((hw, width), lambda i, s: (s[0], 0)),
+            pl.BlockSpec((hw, width), lambda i, s: (1 - s[0], 0)),
+            row, whole(mod.shape), whole(gain.shape),
+        ],
+        [row, row, row],
+        [sds((span, width), F32), sds((span, width), F32), sds((span, width), BF16)],
+        mb=8, us=3, name="post",
+    )
+
+
+def mlp_body(
+    s_ref, n2a_ref, n2b_ref, wa_ref, wb_ref, mod_ref, w1_ref, b1_ref, w2_ref,
+    hid_ref, pre_ref, gm_ref, b1g_ref, b2g_ref,
+):
+    step = pl.program_id(0)
+    first = step < pl.num_programs(0) // 2
+    width = n2a_ref.shape[1]
+    x = jnp.where(first, n2a_ref[...], n2b_ref[...])
+    wtd = jnp.where(first, wa_ref[...], wb_ref[...]).astype(F32)
+    g_mlp = (wtd * mod_ref[0:1, 5 * width : 6 * width]).astype(BF16)
+    gm_ref[...] = g_mlp
+    bias = b1_ref[...].astype(F32)[None, :]
+    hf = w1_ref.shape[1]
+    v = dot(x, w1_ref[...]) + jnp.where(s_ref[0] == 0, bias[:, :hf], bias[:, hf:])
+    gh = dot_nt(g_mlp, w2_ref[...])
+    c0 = 0.7978845608028654
+    c1 = c0 * 0.044715
+    v2 = v * v
+    th = jnp.tanh(v * (c0 + c1 * v2))
+    up = 0.5 + 0.5 * th
+    hid_ref[...] = (v * up).astype(BF16)
+    slope = up + v * (0.5 - 0.5 * (th * th)) * (c0 + 3.0 * c1 * v2)
+    pre = (gh * slope).astype(BF16)
+    pre_ref[...] = pre
+    b1_part = jnp.sum(pre.astype(F32), axis=0, keepdims=True)
+    b2_part = jnp.sum(g_mlp.astype(F32), axis=0, keepdims=True)
+
+    @pl.when(step == 0)
+    def _():
+        b1g_ref[...] = b1_part
+        b2g_ref[...] = b2_part
+
+    @pl.when(step > 0)
+    def _():
+        b1g_ref[...] += b1_part
+        b2g_ref[...] += b2_part
+
+
+def halves(blk, width, n):
+    return [
+        pl.BlockSpec((blk, width), lambda i, s: (jnp.minimum(i, n - 1), 0)),
+        pl.BlockSpec((blk, width), lambda i, s: (jnp.maximum(i - n, 0), 0)),
+    ]
+
+
+def mlp_call(order, n2a, n2b, wa, wb, mod, w1, b1, w2):
+    span, width = n2a.shape
+    hf = w1.shape[1] // 2
+    blk = 256
+    n = span // blk
+    row = lambda w: pl.BlockSpec((blk, w), lambda i, s: (i, 0))
+    return order.call(
+        mlp_body, [n2a, n2b, wa, wb, mod, w1, b1, w2], (2 * n,),
+        halves(blk, width, n) + halves(blk, width, n)
+        + [
+            whole(mod.shape),
+            pl.BlockSpec((width, hf), lambda i, s: (0, s[0])),
+            whole(b1.shape),
+            pl.BlockSpec((hf, width), lambda i, s: (s[0], 0)),
+        ],
+        [row(hf), row(hf), row(width), whole((1, hf)), whole((1, width))],
+        [sds((2 * span, hf), BF16), sds((2 * span, hf), BF16), sds((2 * span, width), BF16),
+         sds((1, hf), F32), sds((1, width), F32)],
+        mb=10, us=9.6, name="mlp",
+    )
+
+
+def store_parts(s_ref, acc_ref, r, keep_ref, send_ref):
+    for i in range(8):
+        rest = sum(((i >> (2 - j)) & 1) * s_ref[6 + j] for j in range(3))
+        for ref, bit in ((keep_ref, s_ref[1]), (send_ref, 1 - s_ref[1])):
+            at = pl.ds(pl.multiple_of((rest + bit * s_ref[5]) * r, 16), r)
+            ref[i // 4, i % 4] = acc_ref[at, :]
+
+
+def wgrad_body(r, s_ref, la_ref, lb_ref, g_ref, keep_ref, send_ref, acc_ref):
+    span = la_ref.shape[0]
+    acc_ref[...] = (dot_tn(la_ref[...], g_ref[:span]) + dot_tn(lb_ref[...], g_ref[span:])).astype(BF16)
+    store_parts(s_ref, acc_ref, r, keep_ref, send_ref)
+
+
+def wgrad_call(order, left_a, left_b, right, blk):
+    rows, cols = left_a.shape[1], right.shape[1]
+    length = right.shape[0]
+    r = rows // 16
+    out = pl.BlockSpec((2, 4, r, blk), lambda i, s: (0, 0, 0, i))
+    return order.call(
+        functools.partial(wgrad_body, r), [left_a, left_b, right], (cols // blk,),
+        [whole(left_a.shape), whole(left_b.shape), pl.BlockSpec((length, blk), lambda i, s: (0, i))],
+        [out] * 2, [sds((2, 4, r, cols), BF16)] * 2,
+        scratch=[pltpu.VMEM((rows, blk), BF16)], mb=8, us=4.2, name="wgrad_fc1",
+    )
+
+
+def wgrad2_body(r, s_ref, lm_ref, lo_ref, g_ref, keep_ref, send_ref, acc_ref):
+    step, n = pl.program_id(0), pl.num_programs(0)
+    mine = lax.div(step, n // 2) == s_ref[0]
+    span = g_ref.shape[0] // 2
+    rows = lm_ref.shape[1]
+    here = pl.ds(pl.multiple_of(step * rows, 128), rows)
+
+    @pl.when(mine)
+    def _():
+        acc_ref[here, :] = dot_tn(lm_ref[...], g_ref[...]).astype(BF16)
+
+    @pl.when(jnp.logical_not(mine))
+    def _():
+        acc_ref[here, :] = (dot_tn(lo_ref[:span], g_ref[span:]) + dot_tn(lo_ref[span:], g_ref[:span])).astype(BF16)
+
+    @pl.when(step == n - 1)
+    def _():
+        store_parts(s_ref, acc_ref, r, keep_ref, send_ref)
+
+
+def wgrad2_call(order, hidden, hidden_o, g_mlp):
+    length, hf = hidden.shape
+    hw = g_mlp.shape[1] // 2
+    r = hf // 8
+    left = pl.BlockSpec((length, 4 * r), lambda i, s: (0, lax.rem(i, 2)))
+    return order.call(
+        functools.partial(wgrad2_body, r), [hidden, hidden_o, g_mlp], (4,),
+        [left, left, pl.BlockSpec((length, hw), lambda i, s: (0, s[0]))],
+        [whole((2, 4, r, hw))] * 2, [sds((2, 4, r, hw), BF16)] * 2,
+        scratch=[pltpu.VMEM((2 * hf, hw), BF16)], mb=16, us=4.5, name="wgrad_fc2",
+    )
+
+
+def fold_body(s_ref, ka, ra, ks, rs, away_ref, stay_ref):
+    away_ref[...] = ka[0] + ra[0]
+    stay_ref[...] = ks[0] + rs[0]
+
+
+def fold_call(order, step, keep, got):
+    _, count, r, n = keep.shape
+    blk = 768 if n % 768 == 0 else 384
+    away = pl.BlockSpec((1, count, r, blk), lambda i, s: (1 - s[step], 0, 0, i))
+    stay = pl.BlockSpec((1, count, r, blk), lambda i, s: (s[step], 0, 0, i))
+    out = pl.BlockSpec((count, r, blk), lambda i, s: (0, 0, i))
+    return order.call(
+        fold_body, [keep, got, keep, got], (n // blk,), [away, away, stay, stay], [out] * 2,
+        [sds((count, r, n), BF16)] * 2, mb=8, us=1.2, name="fold",
+    )
+
+
+def total(refs):
+    out = refs[0][...].astype(F32)
+    for ref in refs[1:]:
+        out = out + ref[...].astype(F32)
+    return out.astype(BF16)
+
+
+def sum_ff_body(s_ref, *refs):
+    one, two, out_ref = refs[:2], refs[2:4], refs[4]
+    r, n = one[0].shape
+    out_ref[:r] = total(one)
+    second = total(two)
+    width = second.shape[1]
+    for q in range(n // width):
+        out_ref[r:, q * width : (q + 1) * width] = second[q * r : (q + 1) * r]
+
+
+def sum_ff_call(order, one, two):
+    r, n = one[0].shape
+    return order.call(
+        sum_ff_body, [*one, *two], (1,), [whole(a.shape) for a in (*one, *two)],
+        [whole((2 * r, n))], [sds((2 * r, n), BF16)], mb=8, us=1.0, name="sum_ff",
+    )[0]
+
+
+def place_ff_body(s_ref, mine_ref, other_ref, fc1_ref, fc2_ref):
+    core = s_ref[0]
+    r, n = fc1_ref.shape[0], mine_ref.shape[1]
+    width = fc2_ref.shape[1] // 2
+    for ref, at in ((mine_ref, core), (other_ref, 1 - core)):
+        fc1_ref[:, pl.ds(pl.multiple_of(at * n, 128), n)] = ref[:r].astype(F32)
+        cols = pl.ds(pl.multiple_of(at * width, 128), width)
+        for q in range(n // width):
+            fc2_ref[q * r : (q + 1) * r, cols] = ref[r:, q * width : (q + 1) * width].astype(F32)
+
+
+def place_ff_call(order, mine, other, hw):
+    r, n = mine.shape[0] // 2, mine.shape[1]
+    shapes = [(r, 2 * n), (r * (n // hw), 2 * hw)]
+    return order.call(
+        place_ff_body, [mine, other], (1,), [whole(mine.shape)] * 2, [whole(x) for x in shapes],
+        [sds(x, F32) for x in shapes], mb=8, us=1.0, name="place_ff",
+    )
+
+
+def sum_att_body(s_ref, *refs):
+    one, two, out_ref = refs[:2], refs[2:4], refs[4]
+    n = one[0].shape[1]
+    out_ref[:, :n] = total(one)
+    out_ref[:, n:] = total(two)
+
+
+def sum_att_call(order, one, two):
+    r, n = one[0].shape
+    shape = (r, n + two[0].shape[1])
+    return order.call(
+        sum_att_body, [*one, *two], (1,), [whole(a.shape) for a in (*one, *two)],
+        [whole(shape)], [sds(shape, BF16)], mb=8, us=1.0, name="sum_att",
+    )[0]
+
+
+def place_att_body(s_ref, mine_ref, other_ref, out_ref, qkv_ref):
+    core = s_ref[0]
+    width = out_ref.shape[1]
+    hw = width // 2
+    for ref, at in ((mine_ref, core), (other_ref, 1 - core)):
+        out_ref[:, pl.ds(pl.multiple_of(at * hw, 128), hw)] = ref[:, :hw].astype(F32)
+        for p in range(hw // 128):
+            for j in range(3):
+                to = pl.ds(pl.multiple_of(j * width + at * hw + p * 128, 128), 128)
+                src = hw + p * 384 + j * 128
+                qkv_ref[:, to] = ref[:, src : src + 128].astype(F32)
+
+
+def place_att_call(order, mine, other, width):
+    r = mine.shape[0]
+    shapes = [(r, width), (r, 3 * width)]
+    return order.call(
+        place_att_body, [mine, other], (1,), [whole(mine.shape)] * 2, [whole(x) for x in shapes],
+        [sds(x, F32) for x in shapes], mb=8, us=1.0, name="place_att",
+    )
+
+
+ROWS = 16
+
+
+def pack_body(s_ref, s1_ref, s2_ref, s3_ref, b1_ref, b2_ref, g1_ref, g2_ref, mod_ref, cond_ref, out_ref):
+    width = s1_ref.shape[1]
+    h = width // 2
+    core = s_ref[0]
+    gain_one, gain_two = g1_ref[...].astype(F32)[None, :], g2_ref[...].astype(F32)[None, :]
+    scale_one = 1.0 + mod_ref[0:1, width : 2 * width]
+    scale_two = 1.0 + mod_ref[0:1, 4 * width : 5 * width]
+    second_one, second_two = s1_ref[1:2, :], s2_ref[1:2, :]
+    rows = [
+        s1_ref[0:1, :], second_one * gain_one, s2_ref[2:3, :],
+        s2_ref[0:1, :], second_two * gain_two, s3_ref[0:1, :],
+    ]
+    gains = [second_one * scale_one, second_two * scale_two]
+    b2 = 0.5 * b2_ref[...]
+    out_ref[...] = jnp.zeros_like(out_ref)
+    nz = out_ref.shape[0] // ROWS
+    per = 12 // nz
+    for z in range(nz):
+        at = z * ROWS
+        for j in range(per):
+            i = per * z + j
+            out_ref[at + j : at + j + 1, :] = rows[i // 2][:, (i % 2) * h : (i % 2 + 1) * h]
+        mine = jnp.where(core == z // (nz // 2), 1.0, 0.0)
+        for j in range(2):
+            i = 2 * (z % (nz // 2)) + j
+            out_ref[at + 3 + j : at + 4 + j, :] = mine * b1_ref[:, i * h : (i + 1) * h]
+        for j in range(4):
+            out_ref[at + 5 + j : at + 6 + j, :] = gains[j // 2][:, (j % 2) * h : (j % 2 + 1) * h]
+        for j in range(2):
+            out_ref[at + 9 + j : at + 10 + j, :] = b2[:, j * h : (j + 1) * h]
+        out_ref[at + 11 : at + 12, 0:128] = 0.5 * cond_ref[...].astype(F32)
+
+
+def pack_call(order, nz, *args):
+    h = args[0].shape[1] // 2
+    return order.call(
+        pack_body, list(args), (1,), [whole(a.shape) for a in args], [whole((nz * ROWS, h))],
+        [sds((nz * ROWS, h), F32)], mb=8, us=1.0, name="pack",
+    )[0]
+
+
+def deal_body(nz, s_ref, a_ref, b_ref, ada_ref, cg_ref, *outs):
+    both = a_ref[...] + b_ref[...]
+    acc = outs[nz]
+    acc[...] = both.reshape(acc.shape)
+    for k in range(nz):
+        outs[k][...] = acc[lax.bitwise_xor(s_ref[9], k)]
+    per = 12 // nz
+    flat = jnp.concatenate([both[z * ROWS + j : z * ROWS + j + 1] for z in range(nz) for j in range(per)], axis=1)
+    high = flat.astype(BF16)
+    rest = flat - high.astype(F32)
+    mid = rest.astype(BF16)
+    low = (rest - mid.astype(F32)).astype(BF16)
+    terms = jnp.concatenate([high.astype(F32), mid.astype(F32), low.astype(F32)] + [jnp.zeros_like(flat)] * 13, axis=0)
+    cg_ref[...] = jnp.sum(dot_nt(terms.astype(BF16), ada_ref[...]), axis=0, keepdims=True)
+
+
+def deal_call(order, nz, mine, got, ada):
+    n = mine.shape[1]
+    return order.call(
+        functools.partial(deal_body, nz), [mine, got, ada], (1,),
+        [whole(mine.shape), whole(mine.shape), whole(ada.shape)],
+        [whole((1, ada.shape[0]))] + [whole((ROWS, n))] * nz,
+        [sds((1, ada.shape[0]), F32)] + [sds((ROWS, n), F32)] * nz,
+        scratch=[pltpu.VMEM((nz, ROWS, n), F32)], mb=8, us=1.0, name="deal",
+    )
+
+
+def last_body(s_ref, *refs):
+    packs, (ada_ref, sum_ref) = refs[:-2], refs[-2:]
+    parts = [ref[k * ROWS : (k + 1) * ROWS] for ref in packs for k in range(ref.shape[0] // ROWS)]
+    whole_sum = parts[0]
+    for part in parts[1:]:
+        whole_sum = whole_sum + part
+    sum_ref[...] = whole_sum
+    cond = jnp.concatenate([part[11:12, 0:128] for part in parts], axis=0)
+    grads = jnp.concatenate([jnp.concatenate([part[j : j + 1] for j in range(3)], axis=1) for part in parts], axis=0)
+    ada_ref[...] = lax.dot_general(
+        cond, grads, (((0,), (0,)), ((), ())), precision=lax.Precision.HIGHEST, preferred_element_type=F32
+    )
+
+
+def last_call(order, packs):
+    n = packs[0].shape[1]
+    return order.call(
+        last_body, packs, (1,), [whole(a.shape) for a in packs], [whole((128, 3 * n)), whole((ROWS, n))],
+        [sds((128, 3 * n), F32), sds((ROWS, n), F32)], mb=8, us=1.0, name="small_last",
+    )
+
+
+def part_body(nt, s_ref, g_ref, w_ref, own_ref, oth_ref):
+    step = pl.program_id(0)
+    half = pl.num_programs(0) // 2
+    part = dot_nt(g_ref[...], w_ref[...]) if nt else dot(g_ref[...], w_ref[...])
+
+    @pl.when(step < half)
+    def _():
+        oth_ref[...] = part.astype(BF16)
+
+    @pl.when(step >= half)
+    def _():
+        own_ref[...] = part
+
+
+def part_call(order, nt, g, w):
+    length, hf = g.shape
+    width = w.shape[0] if nt else w.shape[1]
+    blk = 256
+    n = length // 2 // blk
+    wspec = (
+        pl.BlockSpec((width, hf), lambda i, s: (0, s[0]))
+        if nt
+        else pl.BlockSpec((hf, width), lambda i, s: (s[0], 0))
+    )
+    return order.call(
+        functools.partial(part_body, nt), [g, w], (2 * n,),
+        [pl.BlockSpec((blk, hf), lambda i, s: ((i + n) % (2 * n), 0)), wspec],
+        [
+            pl.BlockSpec((blk, width), lambda i, s: (jnp.maximum(i - n, 0), 0)),
+            pl.BlockSpec((blk, width), lambda i, s: (jnp.minimum(i, n - 1), 0)),
+        ],
+        [sds((length // 2, width), F32), sds((length // 2, width), BF16)],
+        mb=8, us=4.2, name="part",
+    )
+
+
+def norm2_body(s_ref, own_ref, got_ref, mid_ref, br_ref, wtd_ref, mod_ref, gain_ref, gmid_ref, gatt_ref, sum_ref):
+    width = mid_ref.shape[1]
+    g = own_ref[...] + got_ref[...].astype(F32)
+    a_two, inv = layer_stats(mid_ref[...])
+    ga = g * (gain_ref[...].astype(F32)[None, :] * (1.0 + mod_ref[0:1, 4 * width : 5 * width]))
+    gaa = ga * a_two
+    g_mid = wtd_ref[...].astype(F32) + inv * (
+        ga - jnp.mean(ga, -1, keepdims=True) - a_two * jnp.mean(gaa, -1, keepdims=True)
+    )
+    gmid_ref[...] = g_mid
+    gatt_ref[...] = (g_mid * mod_ref[0:1, 2 * width : 3 * width]).astype(BF16)
+    sums = jnp.concatenate(
+        [
+            jnp.sum(g, axis=0, keepdims=True),
+            jnp.sum(g * a_two, axis=0, keepdims=True),
+            jnp.sum(g_mid * br_ref[...], axis=0, keepdims=True),
+        ],
+        axis=0,
+    )
+
+    @pl.when(pl.program_id(0) == 0)
+    def _():
+        sum_ref[...] = jnp.zeros_like(sum_ref)
+
+    sum_ref[0:3, :] += sums
+
+
+def norm2_call(order, own, got, mid, br, wtd, mod, gain):
+    span, width = mid.shape
+    blk = 256
+    row = pl.BlockSpec((blk, width), lambda i, s: (i, 0))
+    return order.call(
+        norm2_body, [own, got, mid, br, wtd, mod, gain], (span // blk,),
+        [row] * 5 + [whole(mod.shape), whole(gain.shape)],
+        [row, row, whole((8, width))],
+        [sds((span, width), F32), sds((span, width), BF16), sds((8, width), F32)],
+        mb=8, us=3, name="norm2",
+    )
+
+
+def oproj_body(r, s_ref, w_ref, ga_ref, gb_ref, am_ref, ao_ref, gt_ref, keep_ref, send_ref, acc_ref):
+    span = ga_ref.shape[0]
+    half = am_ref.shape[0]
+    core = s_ref[0]
+    w = w_ref[...]
+    gt_ref[:, :span] = dot_nt(w, ga_ref[...]).astype(BF16)
+    gt_ref[:, span:] = dot_nt(w, gb_ref[...]).astype(BF16)
+    cols = pl.ds(pl.multiple_of(core * half, 128), half)
+    gac, gbc = ga_ref[:, cols], gb_ref[:, cols]
+    mine = dot(am_ref[:, :span], gac) + dot(am_ref[:, span:], gbc)
+    other = dot(ao_ref[:, span:], gac) + dot(ao_ref[:, :span], gbc)
+    acc_ref[pl.ds(pl.multiple_of(core * half, 16), half), :] = mine.astype(BF16)
+    acc_ref[pl.ds(pl.multiple_of((1 - core) * half, 16), half), :] = other.astype(BF16)
+    store_parts(s_ref, acc_ref, r, keep_ref, send_ref)
+
+
+def oproj_call(order, blocks, out_weight, ga, gb, att_t, att_o):
+    span, width = ga.shape
+    hw = width // 2
+    r = width // 16
+    out = pl.BlockSpec((2, 4, r, hw), lambda i, s: (0, 0, 0, 0))
+    return order.call(
+        functools.partial(oproj_body, r), [out_weight, ga, gb, att_t, att_o], (1,),
+        [pl.BlockSpec((hw, width), lambda i, s: (s[0], 0)), whole(ga.shape), whole(ga.shape),
+         whole(att_t.shape), whole(att_t.shape)],
+        [whole((hw, 2 * span))] + [out] * 2,
+        [sds((hw, 2 * span), BF16)] + [sds((2, 4, r, blocks * hw), BF16)] * 2,
+        scratch=[pltpu.VMEM((width, hw), BF16)], mb=8, us=3, name="oproj",
+    )
+
+
+def norm1_body(s_ref, own_ref, got_ref, tok_ref, gmid_ref, mod_ref, gain_ref, out_ref, sum_ref):
+    width = tok_ref.shape[1]
+    g = own_ref[...] + got_ref[...].astype(F32)
+    a_one, inv = layer_stats(tok_ref[...].astype(F32))
+    ga = g * (gain_ref[...].astype(F32)[None, :] * (1.0 + mod_ref[0:1, width : 2 * width]))
+    gaa = ga * a_one
+    out_ref[...] = (
+        gmid_ref[...]
+        + inv * (ga - jnp.mean(ga, -1, keepdims=True) - a_one * jnp.mean(gaa, -1, keepdims=True))
+    ).astype(BF16)
+
+    @pl.when(pl.program_id(0) == 0)
+    def _():
+        sum_ref[...] = jnp.zeros_like(sum_ref)
+
+    sum_ref[0:1, :] += jnp.sum(g, axis=0, keepdims=True)
+    sum_ref[1:2, :] += jnp.sum(g * a_one, axis=0, keepdims=True)
+
+
+def norm1_call(order, own, got, tok, gmid, mod, gain):
+    span, width = tok.shape
+    blk = 256
+    row = pl.BlockSpec((blk, width), lambda i, s: (i, 0))
+    return order.call(
+        norm1_body, [own, got, tok, gmid, mod, gain], (span // blk,),
+        [row] * 4 + [whole(mod.shape), whole(gain.shape)],
+        [row, whole((8, width))],
+        [sds((span, width), BF16), sds((8, width), F32)],
+        mb=8, us=3, name="norm1",
+    )
+
+
+def dgrad_body(np_, s_ref, *refs):
+    gs, (wq_ref, wk_ref, wv_ref), (own_ref, oth_ref) = refs[:np_], refs[np_ : np_ + 3], refs[np_ + 3 :]
+    step = pl.program_id(0)
+    half = pl.num_programs(0) // 2
+    total = None
+    for j, w_ref in enumerate((wq_ref, wk_ref, wv_ref)):
+        left = jnp.concatenate(
+            [g[:, at + j * 128 : at + (j + 1) * 128] for g in gs for at in range(0, g.shape[1], 384)], axis=1
+        )
+        part = dot_nt(left, w_ref[...])
+        total = part if total is None else total + part
+
+    @pl.when(step < half)
+    def _():
+        oth_ref[...] = total.astype(BF16)
+
+    @pl.when(step >= half)
+    def _():
+        own_ref[...] = total
+
+
+def dgrad_call(order, gs, qkv_weight):
+    length = gs[0].shape[0]
+    width = qkv_weight.shape[0]
+    hw = width // 2
+    blk = 256
+    n = length // 2 // blk
+    wspec = lambda j: pl.BlockSpec((width, hw), lambda i, s: (0, 2 * j + s[0]))
+    return order.call(
+        functools.partial(dgrad_body, len(gs)), [*gs, qkv_weight, qkv_weight, qkv_weight], (2 * n,),
+        [pl.BlockSpec((blk, g.shape[1]), lambda i, s: ((i + n) % (2 * n), 0)) for g in gs]
+        + [wspec(0), wspec(1), wspec(2)],
+        [
+            pl.BlockSpec((blk, width), lambda i, s: (jnp.maximum(i - n, 0), 0)),
+            pl.BlockSpec((blk, width), lambda i, s: (jnp.minimum(i, n - 1), 0)),
+        ],
+        [sds((length // 2, width), F32), sds((length // 2, width), BF16)],
+        mb=8, us=4, name="dgrad",
+    )
+
+
+class Grid:
+    ORDERS = ((1, 2, 4, 8), (2, 1, 8, 4))
+
+    def __init__(self, ndp):
+        self.nz = ndp // 4
+        self.index = lax.axis_index("dp")
+        core = lax.axis_index("ctx")
+        self.flip = lambda mask: [(i, i ^ mask) for i in range(ndp)]
+        masks = [jnp.where(core == 0, a, b) for a, b in zip(*self.ORDERS)]
+        bits = [jnp.where((self.index & m) > 0, 1, 0) for m in masks]
+        self.place = jnp.stack([core, *bits, *masks, self.index // 4]).astype(jnp.int32)
+        self.pairs = [
+            [(2 * i + c, 2 * (i ^ self.ORDERS[c][step]) + c) for i in range(ndp) for c in range(2)] for step in range(4)
+        ]
+
+
+class Job:
+    def __init__(self, pairs):
+        self.pairs, self.step = pairs, 0
+
+    def start(self, keep, send):
+        self.keep = keep
+        self.got = lax.ppermute(send, ("dp", "ctx"), self.pairs[self.step])
+        self.step += 1
+
+    def fold(self, order):
+        shape = self.keep.shape
+        if self.step > 1:
+            shape = (2, shape[0] // 2) + shape[1:]
+        away, stay = fold_call(order, self.step + 1, self.keep.reshape(shape), self.got.reshape(shape))
+        self.start(stay, away)
+
+    def parts(self):
+        return [self.keep[0], self.got[0]]
+
+
+def local_pair(
+    tokens_in, cond_vec, positions, absorbed, cotangent, norm1_gain, qkv_weight, out_weight,
+    norm2_gain, fc1_weight, fc1_bias, fc2_weight, fc2_bias, ada_weight, ada_bias, *, ndp,
+):
+    _, span, width = tokens_in.shape
+    ff_width = fc1_weight.shape[1]
+    hw = width // 2
+    grid = Grid(ndp)
+    nz = grid.nz
+    order = Order(grid.place)
+    swap = lambda v: lax.ppermute(v, "ctx", [(0, 1), (1, 0)])
+
+    tok = tokens_in[0]
+    tok_o = swap(tok)
+    pos_o = swap(positions)
+
+    normed_one, queries, keys, values, cos_t, sin_t, att_t, prob, inverse, mod, wtd = attend_call(
+        order, tok, tok_o, cond_vec, ada_weight, ada_bias, norm1_gain, qkv_weight, positions, pos_o,
+        cotangent[0], absorbed,
+    )
+    wtd_o = swap(wtd)
+    att_o = swap(att_t)
+    middle, branch, n2 = post_call(order, att_t, att_o, out_weight, hbm(tok), mod, norm2_gain)
+    n2_o = swap(n2)
+    hidden, g_pre, g_mlp, b1_sum, b2_sum = mlp_call(
+        order, n2, n2_o, wtd, wtd_o, mod, fc1_weight, fc1_bias, fc2_weight
+    )
+    hidden_o = swap(hidden)
+    fc1, fc2, rest, last = (Job(grid.pairs) for _ in range(4))
+    fc1.start(*wgrad_call(order, n2, n2_o, g_pre, 384))
+    pn_own, pn_oth = part_call(order, True, g_pre, fc1_weight)
+    pn_got = swap(pn_oth)
+    fc2.start(*wgrad2_call(order, hidden, hidden_o, g_mlp))
+    g_mid, g_att, sums2 = norm2_call(
+        order, pn_own, pn_got, middle, branch, wtd, mod, norm2_gain
+    )
+    g_att_o = swap(g_att)
+    g_attn_t, *bufs = oproj_call(
+        order, 3, out_weight, g_att, g_att_o, att_t, att_o
+    )
+
+    fc1.fold(order)
+
+    def back(start, count, old, block, blocks):
+        return attn_bwd(
+            order, start, count, hbm(prob), inverse, g_attn_t, att_t, queries, keys, values, cos_t, sin_t,
+            normed_one, old, block, blocks,
+        )
+
+    pairs = hw // 128
+    g_a, *bufs = back(0, pairs - 1, bufs, 1, pairs)
+    rest.start(*bufs)
+    fc2.fold(order)
+    fc1.fold(order)
+    g_b, *bufs = back(pairs - 1, 1, None, 0, 1)
+    last.start(*bufs)
+    fc2.fold(order)
+    fc1.fold(order)
+    rest.fold(order)
+    d_own, d_oth = dgrad_call(order, [g_a, g_b], qkv_weight)
+    d_got = swap(d_oth)
+    last.fold(order)
+    fc2.fold(order)
+    rest.fold(order)
+    pm_own, pm_oth = part_call(order, False, hidden, fc2_weight)
+    pm_got = swap(pm_oth)
+    last.fold(order)
+    rest.fold(order)
+    input_grad, sums1 = norm1_call(order, d_own, d_got, tok, g_mid, mod, norm1_gain)
+    mixed, sums3 = mix_call(order, pm_own, pm_got, middle, wtd, mod, fc2_bias)
+    packet = pack_call(
+        order, nz, sums1, sums2, sums3, b1_sum, b2_sum, norm1_gain, norm2_gain, mod, cond_vec
+    )
+    packet_o = swap(packet)
+    last.fold(order)
+    ff = sum_ff_call(order, fc1.parts(), fc2.parts())
+    ff_o = swap(ff)
+    cond_grad, *deals = deal_call(order, nz, packet, packet_o, ada_weight)
+    deals = [deals[0]] + [lax.ppermute(deals[k], "dp", grid.flip(4 * k)) for k in range(1, nz)]
+    att = sum_att_call(order, rest.parts(), last.parts())
+    att_o2 = swap(att)
+    fc1_grad, fc2_grad = place_ff_call(order, ff, ff_o, hw)
+    deals = jnp.concatenate(deals, 0)
+    packs = [deals] + [lax.ppermute(deals, "dp", grid.flip(mask)) for mask in (1, 2, 3)]
+    out_grad, qkv_grad = place_att_call(order, att, att_o2, width)
+    ada_part, sums = last_call(order, packs)
+
+    na, nb, nc = 6 * width // ndp, width // ndp, ff_width // ndp
+    inner = lax.rem(grid.index, 4)
+    take = lambda v, start, n: lax.dynamic_slice_in_dim(v, start, n, v.ndim - 1)
+    ada_grad = take(ada_part, inner * na, na)
+    ada_bias_grad = take(sums[0:3].reshape(-1), inner * na, na)
+    fc1_bias_grad = take(sums[3:5].reshape(-1), inner * nc, nc)
+    norm1_grad = take(sums[5:7].reshape(-1), grid.index * nb, nb)
+    norm2_grad = take(sums[7:9].reshape(-1), grid.index * nb, nb)
+    fc2_bias_grad = take(sums[9:11].reshape(-1), grid.index * nb, nb)
+    return (
+        mixed[None], input_grad[None], cond_grad, norm1_grad, qkv_grad, out_grad, norm2_grad,
+        fc1_grad, fc1_bias_grad, fc2_grad, fc2_bias_grad, ada_grad, ada_bias_grad,
+    )
 
 
 def layer_norm(stream):
@@ -77,7 +1065,7 @@
     return (probability, grad_scores)
 
 
-def local(
+def local_any(
     tokens_in,
     cond_vec,
     positions,
@@ -345,6 +1333,13 @@
     return (mixed, input_grad, cond_grad) + tuple(summed)
 
 
+def local(*args, ndp, nctx):
+    seqs, span, _ = args[0].shape
+    if nctx == 2 and seqs == 1 and ndp == 16 and span == 512:
+        return local_pair(*args, ndp=ndp)
+    return local_any(*args)
+
+
 def solution(mesh):
     in_specs = (
         P("dp", "ctx", None),
@@ -378,4 +1373,5 @@
         P(None, "dp"),
         P("dp"),
     )
-    return jax.shard_map(local, mesh=mesh, in_specs=in_specs, out_specs=out_specs, check_vma=False)
+    step = functools.partial(local, ndp=mesh.shape["dp"], nctx=mesh.shape["ctx"])
+    return jax.shard_map(step, mesh=mesh, in_specs=in_specs, out_specs=out_specs, check_vma=False)

time: 1090 us -> 175 us (0.16)
  waiting for transfers between devices: 654 us -> 18.6 us
  matrix products: 190 us -> 0 us
  Pallas kernels: 0 us -> 108 us
  blocking collectives: 94.7 us -> 0 us
  local copies, waits for them, and re-layouts: 74.8 us -> 4.12 us
  other arithmetic: 47.2 us -> 0 us
  starting transfers between devices: 1.11 us -> 42.6 us
  between operations: 17 us -> 1.07 us
    reduce_scatter x5 -> x0, waiting for transfers between devices: 647 us -> none  [the longest x1 177 us: local(): lax.psum_scatter(grad_fc2, 'dp', scatter_dimension=0, tiled=True)]
    dot_general x28 -> x0, matrix products: 190 us -> none  [the longest x4 28.5 us: score_grads(): jnp.einsum('sqhd,skhd->sqhk', query_blk, key_blk, preferred_element_type=...]
    pallas_call x0 -> x33, Pallas kernels: none -> 108 us  [call(): pl.pallas_call(inner, grid_spec=pltpu.PrefetchScalarGridSpec(num_scalar_p...]
    unnamed x1 -> x0, blocking collectives: 76.1 us -> none
    ppermute x0 -> x35, starting transfers between devices: none -> 42.6 us  [the longest x16 30.9 us: start(): self.got = lax.ppermute(send, ('dp', 'ctx'), self.pairs[self.step])]
    unnamed x168 -> x26, local copies, waits for them, and re-layouts: 29.7 us -> 0.83 us
    ppermute x0 -> x35, waiting for transfers between devices: none -> 18.6 us  [the longest x16 7.55 us: start(): self.got = lax.ppermute(send, ('dp', 'ctx'), self.pairs[self.step])]
    reduce_sum x10 -> x0, other arithmetic: 15.8 us -> none  [the longest x3 7.55 us: pre_norm(): layer_norm(stream) * norm_gain * (1.0 + scale_vec[:, None, :])]
  transfers between devices with their start and end apart: 10 -> 35, of which waited for: 6 -> 14; matrix products, arithmetic and copies ran while one was open for 24% -> 0% of each run, Pallas kernels for 0% -> 43%
where the time goes in v2:
time: 175 us
  Pallas kernels  108 us (62%)
  starting transfers between devices  42.6 us (24%)
  waiting for transfers between devices  18.6 us (11%)
  local copies, waits for them, and re-layouts  4.12 us (2%)
    pallas_call x33, Pallas kernels, call(): pl.pallas_call(inner, grid_spec=pltpu.PrefetchScalarGridSpec(num_scalar_p...  108 us
    ppermute x16, starting transfers between devices, start(): self.got = lax.ppermute(send, ('dp', 'ctx'), self.pairs[self.step])  30.9 us
    ppermute x16, waiting for transfers between devices, start(): self.got = lax.ppermute(send, ('dp', 'ctx'), self.pairs[self.step])  7.55 us
    ppermute x13, waiting for transfers between devices, local_pair(): swap = lambda v: lax.ppermute(v, 'ctx', [(0, 1), (1, 0)])  6.56 us
    ppermute x3, starting transfers between devices, local_pair(): lax.ppermute(deals, 'dp', grid.flip(mask))  4.68 us
    ppermute x3, starting transfers between devices, local_pair(): lax.ppermute(deals[k], 'dp', grid.flip(4 * k))  4.43 us
  transfers between devices with their start and end apart: 35, of which 14 were waited for; matrix products, arithmetic and copies ran while one was open for 0% of the time, Pallas kernels for 43%

profile of v2, /device:TPU:0, one launch (start us, length us, event | category | flops | bytes accessed | tf_op | source)
XLA Modules:
  0.0 174.9 jit_solution(8238059846751473026)
XLA Ops:
  1.3 2.0 %collective-permute-done.1.refs_11_ = s32[1,512]{1,0:T(1,128)S(1)} collective-permute-done((s32[1,512]{1,0:T(1,128)}, s32[1,512]{1,0:T(1,128)S(1)}, u32[]{:S(2)}, u32[]{:S(2)}) %collective-permute-start.1) | collective-permute-done | bytes 2080 | tf_op jit(solution)/shard_map/ppermute | solution.py:911
  3.3 23.0 %attend.1 = (bf16[1024,768]{1,0:T(8,128)(2,1)S(1)}, bf16[1024,384]{1,0:T(8,128)(2,1)S(1)}, bf16[1024,384]{1,0:T(8,128)(2,1)S(1)}, bf16[1024,384]{1,0:T(8,128)(2,...) custom-call(s32[10]{0:T(128)S(1)} %stack.43.refs_0_, ...), custom_call_target="tpu_custom_call" | custom-call | flops 4000000000 | bytes 65536 | tf_op jit(solution)/shard_map/attend/pallas_call | solution.py:55
  26.8 1.8 %collective-permute-done.2.refs_2_.refs_5_ = bf16[384,1024]{1,0:T(8,128)(2,1)S(1)} collective-permute-done((bf16[384,1024]{1,0:T(8,128)(2,1)S(1)}, bf16[384,1024]{1,0:T(8,128)(2,1)S(1)}, u32[]{:S(2)}, u32[]{:S(2)}) %collective-permute-start.2) | collective-permute-done | bytes 786464 | tf_op jit(solution)/shard_map/ppermute | solution.py:911
  28.6 3.6 %post.1 = (f32[512,768]{1,0:T(8,128)S(1)}, f32[512,768]{1,0:T(8,128)S(1)}, bf16[512,768]{1,0:T(8,128)(2,1)S(1)}, f32[8,128]{1,0:T(8,128)S(1)}) custom-call(s32[10]{0:T(128)S(1)} %stack.43.refs_0_, bf16[384,1024]{1,0:T(8,128)(2,1)S(1)} %get-tuple-element.128.refs_1_.refs_4_, bf16[384,1024]{1,0:T(8,128)(2,1)S(1)} %collective-permute-done.2.refs_2_.refs_5_, ...), custom_call_target="tpu_custom_call" | custom-call | flops 600000000 | bytes 65536 | tf_op jit(solution)/shard_map/post/pallas_call | solution.py:55
  32.6 1.9 %collective-permute-done.3.refs_2_ = bf16[512,768]{1,0:T(8,128)(2,1)S(1)} collective-permute-done((bf16[512,768]{1,0:T(8,128)(2,1)S(1)}, bf16[512,768]{1,0:T(8,128)(2,1)S(1)}, u32[]{:S(2)}, u32[]{:S(2)}) %collective-permute-start.3) | collective-permute-done | bytes 786464 | tf_op jit(solution)/shard_map/ppermute | solution.py:911
  34.6 8.1 %mlp.1 = (bf16[1024,1536]{1,0:T(8,128)(2,1)S(1)}, bf16[1024,1536]{1,0:T(8,128)(2,1)S(1)}, bf16[1024,768]{1,0:T(8,128)(2,1)S(1)}, f32[1,1536]{1,0:T(1,128)S(1)}, ...) custom-call(s32[10]{0:T(128)S(1)} %stack.43.refs_0_, bf16[512,768]{1,0:T(8,128)(2,1)S(1)} %get-tuple-element.131.refs_1_, ...), custom_call_target="tpu_custom_call" | custom-call | flops 1920000000 | bytes 65536 | tf_op jit(solution)/shard_map/mlp/pallas_call | solution.py:55
  43.1 5.5 %wgrad_fc1.1 = (bf16[2,4,48,1536]{3,2,1,0:T(8,128)(2,1)S(1)}, bf16[2,4,48,1536]{3,2,1,0:T(8,128)(2,1)S(1)}, f32[8,128]{1,0:T(8,128)S(1)}) custom-call(s32[10]{0:T(128)S(1)} %stack.43.refs_0_, bf16[512,768]{1,0:T(8,128)(2,1)S(1)} %get-tuple-element.131.refs_1_, bf16[512,768]{1,0:T(8,128)(2,1)S(1)} %collective-permute-done.3.refs_2_, ...), custom_call_target="tpu_custom_call" | custom-call | flops 840000000 | bytes 65536 | tf_op jit(solution)/shard_map/wgrad_fc1/pallas_call | solution.py:55
  48.5 4.2 %part.2 = (f32[512,768]{1,0:T(8,128)S(1)}, bf16[512,768]{1,0:T(8,128)(2,1)S(1)}, f32[8,128]{1,0:T(8,128)S(1)}) custom-call(s32[10]{0:T(128)S(1)} %stack.43.refs_0_, bf16[1024,1536]{1,0:T(8,128)(2,1)S(1)} %get-tuple-element.137.refs_3_.refs_1_, bf16[768,3072]{1,0:T(8,128)(2,1)S(1)} %copy-done.1, f32[8,128]{1,0:T(8,128)S(1)} %get-tuple-element.139.refs_3_), custom_call_target="tpu_custom_call" | custom-call | flops 840000000 | bytes 65536 | tf_op jit(solution)/shard_map/part/pallas_call | solution.py:55
  53.0 2.8 %collective-permute-start.8 = (bf16[2,4,48,1536]{3,2,1,0:T(8,128)(2,1)S(1)}, bf16[2,4,48,1536]{3,2,1,0:T(8,128)(2,1)S(1)}, u32[]{:S(2)}, u32[]{:S(2)}) collective-permute-start(bf16[2,4,48,1536]{3,2,1,0:T(8,128)(2,1)S(1)} %get-tuple-element.159), channel_id=1, source_target_pairs={{0,2},{1,5},{2,0},{3,7},{4,6},{5,1},{6,4},{7,3},{8,10},{9,13},{10,... | collective-permute-start | bytes 3538952 | tf_op jit(solution)/shard_map/ppermute | solution.py:887
  55.8 6.0 %wgrad_fc2.1 = (bf16[2,4,192,384]{3,2,1,0:T(8,128)(2,1)S(1)}, bf16[2,4,192,384]{3,2,1,0:T(8,128)(2,1)S(1)}, f32[8,128]{1,0:T(8,128)S(1)}) custom-call(s32[10]{0:T(128)S(1)} %stack.43.refs_0_, bf16[1024,1536]{1,0:T(8,128)(2,1)S(1)} %get-tuple-element.134.refs_1_, bf16[1024,1536]{1,0:T(8,128)(2,1)S(1)} %collective-permute-done.6.refs_2_, ...), custom_call_target="tpu_custom_call" | custom-call | flops 900000000 | bytes 65536 | tf_op jit(solution)/shard_map/wgrad_fc2/pallas_call | solution.py:55
  61.9 2.1 %norm2.1 = (f32[512,768]{1,0:T(8,128)S(1)}, bf16[512,768]{1,0:T(8,128)(2,1)S(1)}, f32[8,768]{1,0:T(8,128)S(1)}, f32[8,128]{1,0:T(8,128)S(1)}) custom-call(s32[10]{0:T(128)S(1)} %stack.43.refs_0_, f32[512,768]{1,0:T(8,128)S(1)} %get-tuple-element.140.refs_1_, bf16[512,768]{1,0:T(8,128)(2,1)S(1)} %collective-permute-done.5.refs_2_, ...), custom_call_target="tpu_custom_call" | custom-call | flops 600000000 | bytes 65536 | tf_op jit(solution)/shard_map/norm2/pallas_call | solution.py:55
  66.3 2.3 %oproj.1 = (bf16[384,1024]{1,0:T(8,128)(2,1)S(1)}, bf16[2,4,48,1152]{3,2,1,0:T(8,128)(2,1)S(1)}, bf16[2,4,48,1152]{3,2,1,0:T(8,128)(2,1)S(1)}, f32[8,128]{1,0:T(8,128)S(1)}) custom-call(s32[10]{0:T(128)S(1)} %stack.43.refs_0_, bf16[768,768]{1,0:T(8,128)(2,1)S(1)} %copy-done.3, bf16[512,768]{1,0:T(8,128)(2,1)S(1)} %get-tuple-element.147.refs_2_, ...), custom_call_target="tpu_custom_call" | custom-call | flops 600000000 | bytes 65536 | tf_op jit(solution)/shard_map/oproj/pallas_call | solution.py:55
  71.1 2.1 %collective-permute-start.10 = (bf16[4,48,1536]{2,1,0:T(8,128)(2,1)S(1)}, bf16[4,48,1536]{2,1,0:T(8,128)(2,1)S(1)}, u32[]{:S(2)}, u32[]{:S(2)}) collective-permute-start(bf16[4,48,1536]{2,1,0:T(8,128)(2,1)S(1)} %get-tuple-element.165), channel_id=1, source_target_pairs={{0,4},{1,3},{2,6},{3,1},{4,0},{5,7},{6,2},{7,5},{8,12},{9,11},{10,... | collective-permute-start | bytes 1769480 | tf_op jit(solution)/shard_map/ppermute | solution.py:887
  73.2 15.6 %attn_bwd.2 = (bf16[1024,768]{1,0:T(8,128)(2,1)S(1)}, bf16[2,4,48,1152]{3,2,1,0:T(8,128)(2,1)S(1)}, bf16[2,4,48,1152]{3,2,1,0:T(8,128)(2,1)S(1)}, f32[8,128]{1,0:T(8,128)S(1)}) custom-call(s32[10]{0:T(128)S(1)} %stack.43.refs_0_, bf16[6,1024,1024]{2,1,0:T(8,128)(2,1)} %get-tuple-element.135.refs_1_, ...), custom_call_target="tpu_custom_call", output_to_operand_aliasing={{1}: (11, {}), {2}: (12, {})} | custom-call | flops 3200000000 | bytes 65536 | tf_op jit(solution)/shard_map/attn_bwd/pallas_call | solution.py:55
  88.8 1.6 collective-permute-start.9
  92.7 1.6 collective-permute-start.12
  94.4 8.8 %attn_bwd.3 = (bf16[1024,384]{1,0:T(8,128)(2,1)S(1)}, bf16[2,4,48,384]{3,2,1,0:T(8,128)(2,1)S(1)}, bf16[2,4,48,384]{3,2,1,0:T(8,128)(2,1)S(1)}, f32[8,128]{1,0:T(8,128)S(1)}) custom-call(s32[10]{0:T(128)S(1)} %stack.43.refs_0_, bf16[6,1024,1024]{2,1,0:T(8,128)(2,1)} %get-tuple-element.135.refs_1_, f32[3,8,1024]{2,1,0:T(8,128)S(1)} %get-tuple-element.136.refs_2_, ...), custom_call_target="tpu_custom_call" | custom-call | flops 1600000000 | bytes 65536 | tf_op jit(solution)/shard_map/attn_bwd/pallas_call | solution.py:55
  103.2 3.0 %collective-permute-done.13 = bf16[4,192,384]{2,1,0:T(8,128)(2,1)S(1)} collective-permute-done((bf16[4,192,384]{2,1,0:T(8,128)(2,1)S(1)}, bf16[4,192,384]{2,1,0:T(8,128)(2,1)S(1)}, u32[]{:S(2)}, u32[]{:S(2)}) %collective-permute-start.13) | collective-permute-done | bytes 589856 | tf_op jit(solution)/shard_map/ppermute | solution.py:887
  111.4 1.6 collective-permute-start.15
  113.0 4.2 %dgrad.1 = (f32[512,768]{1,0:T(8,128)S(1)}, bf16[512,768]{1,0:T(8,128)(2,1)S(1)}, f32[8,128]{1,0:T(8,128)S(1)}) custom-call(s32[10]{0:T(128)S(1)} %stack.43.refs_0_, bf16[1024,768]{1,0:T(8,128)(2,1)S(1)} %get-tuple-element.184.refs_1_, bf16[1024,384]{1,0:T(8,128)(2,1)S(1)} %get-tuple-element.185.refs_2_, bf16[768,2304]{1,0:T(8,128)(2,1)S(1)} %copy-done, ...), custom_call_target="tpu_custom_call" | custom-call | flops 800000000 | bytes 65536 | tf_op jit(solution)/shard_map/dgrad/pallas_call | solution.py:55
  121.8 3.9 %part.3 = (f32[512,768]{1,0:T(8,128)S(1)}, bf16[512,768]{1,0:T(8,128)(2,1)S(1)}, f32[8,128]{1,0:T(8,128)S(1)}) custom-call(s32[10]{0:T(128)S(1)} %stack.43.refs_0_, bf16[1024,1536]{1,0:T(8,128)(2,1)S(1)} %get-tuple-element.134.refs_1_, bf16[3072,768]{1,0:T(8,128)(2,1)S(1)} %copy-done.2, f32[8,128]{1,0:T(8,128)S(1)} %get-tuple-element.190.refs_3_), custom_call_target="tpu_custom_call" | custom-call | flops 840000000 | bytes 65536 | tf_op jit(solution)/shard_map/part/pallas_call | solution.py:55
  127.6 4.7 %collective-permute-start.22 = (bf16[1,48,1536]{2,1,0:T(8,128)(2,1)S(1)}, bf16[1,48,1536]{2,1,0:T(8,128)(2,1)S(1)}, u32[]{:S(2)}, u32[]{:S(2)}) collective-permute-start(bf16[1,48,1536]{2,1,0:T(8,128)(2,1)S(1)} %get-tuple-element.214), channel_id=1, source_target_pairs={{0,16},{1,9},{2,18},{3,11},{4,20},{5,13},{6,22},{7,15},{8,24},{9,1... | collective-permute-start | bytes 442376 | tf_op jit(solution)/shard_map/ppermute | solution.py:887
  132.4 3.8 %collective-permute-start.23 = (bf16[1,192,384]{2,1,0:T(8,128)(2,1)S(1)}, bf16[1,192,384]{2,1,0:T(8,128)(2,1)S(1)}, u32[]{:S(2)}, u32[]{:S(2)}) collective-permute-start(bf16[1,192,384]{2,1,0:T(8,128)(2,1)S(1)} %get-tuple-element.216), channel_id=1, source_target_pairs={{0,16},{1,9},{2,18},{3,11},{4,20},{5,13},{6,22},{7,15},{8,24},{9,1... | collective-permute-start | bytes 442376 | tf_op jit(solution)/shard_map/ppermute | solution.py:887
  137.8 2.6 %norm1.1 = (bf16[512,768]{1,0:T(8,128)(2,1)}, f32[8,768]{1,0:T(8,128)S(1)}, f32[8,128]{1,0:T(8,128)S(1)}) custom-call(s32[10]{0:T(128)S(1)} %stack.43.refs_0_, f32[512,768]{1,0:T(8,128)S(1)} %get-tuple-element.193.refs_1_, bf16[512,768]{1,0:T(8,128)(2,1)S(1)} %collective-permute-done.18.refs_2_, bf16[512,768]{1,0:T(8,128)(2,1)S(1)} %bitcast.41, ...), custom_call_target="tpu_custom_call" | custom-call | flops 600000000 | bytes 65536 | tf_op jit(solution)/shard_map/norm1/pallas_call | solution.py:55
  140.5 1.8 %mix.1 = (bf16[512,768]{1,0:T(8,128)(2,1)}, f32[8,768]{1,0:T(8,128)S(1)}, f32[8,128]{1,0:T(8,128)S(1)}) custom-call(s32[10]{0:T(128)S(1)} %stack.43.refs_0_, f32[512,768]{1,0:T(8,128)S(1)} %get-tuple-element.191.refs_1_, bf16[512,768]{1,0:T(8,128)(2,1)S(1)} %collective-permute-done.17.refs_2_, f32[512,768]{1,0:T(8,128)S(1)} %get-tuple-element.142.refs_3_, ...), custom_call_target="tpu_custom_call" | custom-call | flops 500000000 | bytes 65536 | tf_op jit(solution)/shard_map/mix/pallas_call | solution.py:55
  142.9 6.6 %collective-permute-start.31 = (bf16[1,48,1152]{2,1,0:T(8,128)(2,1)S(1)}, bf16[1,48,1152]{2,1,0:T(8,128)(2,1)S(1)}, u32[]{:S(2)}, u32[]{:S(2)}) collective-permute-start(bf16[1,48,1152]{2,1,0:T(8,128)(2,1)S(1)} %get-tuple-element.228), channel_id=1, source_target_pairs={{0,16},{1,9},{2,18},{3,11},{4,20},{5,13},{6,22},{7,15},{8,24},{9,1... | collective-permute-start | bytes 331784 | tf_op jit(solution)/shard_map/ppermute | solution.py:887
  150.9 1.5 deal.1
  153.7 1.6 collective-permute-start.26
  155.3 1.5 collective-permute-start.27
  158.5 2.3 %collective-permute-done.27 = f32[16,384]{1,0:T(8,128)S(1)} collective-permute-done((f32[16,384]{1,0:T(8,128)S(1)}, f32[16,384]{1,0:T(8,128)S(1)}, u32[]{:S(2)}, u32[]{:S(2)}) %collective-permute-start.27) | collective-permute-done | bytes 24608 | tf_op jit(solution)/shard_map/ppermute | solution.py:979
  160.9 2.5 %collective-permute-start.28 = (f32[64,384]{1,0:T(8,128)S(1)}, f32[64,384]{1,0:T(8,128)S(1)}, u32[]{:S(2)}, u32[]{:S(2)}) collective-permute-start(f32[64,384]{1,0:T(8,128)S(1)} %constant_dynamic-update-slice_fusion.refs_1_), channel_id=1, source_target_pairs={{0,2},{2,0},{4,6},{6,4},{8,10},{10,8},{12,14},{14,12},{16,18},{18,... | collective-permute-start | bytes 294920 | tf_op jit(solution)/shard_map/ppermute | solution.py:984
  165.6 1.6 place_ff.1
  (112 shorter events, 37.6 us)
Async XLA Ops:
  0.6 2.6 %collective-permute-start = (bf16[512,768]{1,0:T(8,128)(2,1)}, bf16[512,768]{1,0:T(8,128)(2,1)S(1)}, u32[]{:S(2)}, u32[]{:S(2)}) collective-permute-start(bf16[512,768]{1,0:T(8,128)(2,1)} %bitcast.38), channel_id=1, source_target_pairs={{0,1},{1,0},{2,3},{3,2},{4,5},{5,4},{6,7},{7,6},{8,9},{9,8},{10,11... | collective-permute-start | bytes 2359304 | tf_op jit(solution)/shard_map/ppermute | solution.py:911
  26.6 6.0 %collective-permute-start.4 = (bf16[512,768]{1,0:T(8,128)(2,1)S(1)}, bf16[512,768]{1,0:T(8,128)(2,1)S(1)}, u32[]{:S(2)}, u32[]{:S(2)}) collective-permute-start(bf16[512,768]{1,0:T(8,128)(2,1)S(1)} %get-tuple-element.132.refs_3_.refs_5_.refs_4_), channel_id=1, source_target_pairs={{0,1},{1,0},{2,3},{3,2},{4,5},{5,4},{6,7},{7,6},{8,9},{9,8},{10,11... | collective-permute-start | bytes 2359304 | tf_op jit(solution)/shard_map/ppermute | solution.py:911
  32.2 2.4 %collective-permute-start.3 = (bf16[512,768]{1,0:T(8,128)(2,1)S(1)}, bf16[512,768]{1,0:T(8,128)(2,1)S(1)}, u32[]{:S(2)}, u32[]{:S(2)}) collective-permute-start(bf16[512,768]{1,0:T(8,128)(2,1)S(1)} %get-tuple-element.131.refs_1_), channel_id=1, source_target_pairs={{0,1},{1,0},{2,3},{3,2},{4,5},{5,4},{6,7},{7,6},{8,9},{9,8},{10,11... | collective-permute-start | bytes 2359304 | tf_op jit(solution)/shard_map/ppermute | solution.py:911
  42.6 13.2 %collective-permute-start.6 = (bf16[1024,1536]{1,0:T(8,128)(2,1)S(1)}, bf16[1024,1536]{1,0:T(8,128)(2,1)S(1)}, u32[]{:S(2)}, u32[]{:S(2)}) collective-permute-start(bf16[1024,1536]{1,0:T(8,128)(2,1)S(1)} %get-tuple-element.134.refs_1_), channel_id=1, source_target_pairs={{0,1},{1,0},{2,3},{3,2},{4,5},{5,4},{6,7},{7,6},{8,9},{9,8},{10,11... | collective-permute-start | bytes 9437192 | tf_op jit(solution)/shard_map/ppermute | solution.py:911
  52.8 9.1 %collective-permute-start.5 = (bf16[512,768]{1,0:T(8,128)(2,1)S(1)}, bf16[512,768]{1,0:T(8,128)(2,1)S(1)}, u32[]{:S(2)}, u32[]{:S(2)}) collective-permute-start(bf16[512,768]{1,0:T(8,128)(2,1)S(1)} %get-tuple-element.141), channel_id=1, source_target_pairs={{0,1},{1,0},{2,3},{3,2},{4,5},{5,4},{6,7},{7,6},{8,9},{9,8},{10,11... | collective-permute-start | bytes 2359304 | tf_op jit(solution)/shard_map/ppermute | solution.py:911
  53.0 17.0 %collective-permute-start.8 = (bf16[2,4,48,1536]{3,2,1,0:T(8,128)(2,1)S(1)}, bf16[2,4,48,1536]{3,2,1,0:T(8,128)(2,1)S(1)}, u32[]{:S(2)}, u32[]{:S(2)}) collective-permute-start(bf16[2,4,48,1536]{3,2,1,0:T(8,128)(2,1)S(1)} %get-tuple-element.159), channel_id=1, source_target_pairs={{0,2},{1,5},{2,0},{3,7},{4,6},{5,1},{6,4},{7,3},{8,10},{9,13},{10,... | collective-permute-start | bytes 3538952 | tf_op jit(solution)/shard_map/ppermute | solution.py:887
  64.0 26.3 %collective-permute-start.11 = (bf16[2,4,192,384]{3,2,1,0:T(8,128)(2,1)S(1)}, bf16[2,4,192,384]{3,2,1,0:T(8,128)(2,1)S(1)}, u32[]{:S(2)}, u32[]{:S(2)}) collective-permute-start(bf16[2,4,192,384]{3,2,1,0:T(8,128)(2,1)S(1)} %get-tuple-element.167), channel_id=1, source_target_pairs={{0,2},{1,5},{2,0},{3,7},{4,6},{5,1},{6,4},{7,3},{8,10},{9,13},{10,... | collective-permute-start | bytes 3538952 | tf_op jit(solution)/shard_map/ppermute | solution.py:887
  71.1 20.8 %collective-permute-start.10 = (bf16[4,48,1536]{2,1,0:T(8,128)(2,1)S(1)}, bf16[4,48,1536]{2,1,0:T(8,128)(2,1)S(1)}, u32[]{:S(2)}, u32[]{:S(2)}) collective-permute-start(bf16[4,48,1536]{2,1,0:T(8,128)(2,1)S(1)} %get-tuple-element.165), channel_id=1, source_target_pairs={{0,4},{1,3},{2,6},{3,1},{4,0},{5,7},{6,2},{7,5},{8,12},{9,11},{10,... | collective-permute-start | bytes 1769480 | tf_op jit(solution)/shard_map/ppermute | solution.py:887
  88.8 19.4 %collective-permute-start.9 = (bf16[2,4,48,1152]{3,2,1,0:T(8,128)(2,1)S(1)}, bf16[2,4,48,1152]{3,2,1,0:T(8,128)(2,1)S(1)}, u32[]{:S(2)}, u32[]{:S(2)}) collective-permute-start(bf16[2,4,48,1152]{3,2,1,0:T(8,128)(2,1)S(1)} %get-tuple-element.163), channel_id=1, source_target_pairs={{0,2},{1,5},{2,0},{3,7},{4,6},{5,1},{6,4},{7,3},{8,10},{9,13},{10,... | collective-permute-start | bytes 2654216 | tf_op jit(solution)/shard_map/ppermute | solution.py:887
  91.1 15.2 %collective-permute-start.13 = (bf16[4,192,384]{2,1,0:T(8,128)(2,1)S(1)}, bf16[4,192,384]{2,1,0:T(8,128)(2,1)S(1)}, u32[]{:S(2)}, u32[]{:S(2)}) collective-permute-start(bf16[4,192,384]{2,1,0:T(8,128)(2,1)S(1)} %get-tuple-element.173), channel_id=1, source_target_pairs={{0,4},{1,3},{2,6},{3,1},{4,0},{5,7},{6,2},{7,5},{8,12},{9,11},{10,... | collective-permute-start | bytes 1769480 | tf_op jit(solution)/shard_map/ppermute | solution.py:887
  92.7 14.2 %collective-permute-start.12 = (bf16[2,48,1536]{2,1,0:T(8,128)(2,1)S(1)}, bf16[2,48,1536]{2,1,0:T(8,128)(2,1)S(1)}, u32[]{:S(2)}, u32[]{:S(2)}) collective-permute-start(bf16[2,48,1536]{2,1,0:T(8,128)(2,1)S(1)} %get-tuple-element.171), channel_id=1, source_target_pairs={{0,8},{1,17},{2,10},{3,19},{4,12},{5,21},{6,14},{7,23},{8,0},{9,25... | collective-permute-start | bytes 884744 | tf_op jit(solution)/shard_map/ppermute | solution.py:887
  109.4 11.4 %collective-permute-start.14 = (bf16[4,48,1152]{2,1,0:T(8,128)(2,1)S(1)}, bf16[4,48,1152]{2,1,0:T(8,128)(2,1)S(1)}, u32[]{:S(2)}, u32[]{:S(2)}) collective-permute-start(bf16[4,48,1152]{2,1,0:T(8,128)(2,1)S(1)} %get-tuple-element.179), channel_id=1, source_target_pairs={{0,4},{1,3},{2,6},{3,1},{4,0},{5,7},{6,2},{7,5},{8,12},{9,11},{10,... | collective-permute-start | bytes 1327112 | tf_op jit(solution)/shard_map/ppermute | solution.py:887
  110.5 8.0 %collective-permute-start.16 = (bf16[2,4,48,384]{3,2,1,0:T(8,128)(2,1)S(1)}, bf16[2,4,48,384]{3,2,1,0:T(8,128)(2,1)S(1)}, u32[]{:S(2)}, u32[]{:S(2)}) collective-permute-start(bf16[2,4,48,384]{3,2,1,0:T(8,128)(2,1)S(1)} %get-tuple-element.183), channel_id=1, source_target_pairs={{0,2},{1,5},{2,0},{3,7},{4,6},{5,1},{6,4},{7,3},{8,10},{9,13},{10,... | collective-permute-start | bytes 884744 | tf_op jit(solution)/shard_map/ppermute | solution.py:887
  111.4 8.8 %collective-permute-start.15 = (bf16[2,192,384]{2,1,0:T(8,128)(2,1)S(1)}, bf16[2,192,384]{2,1,0:T(8,128)(2,1)S(1)}, u32[]{:S(2)}, u32[]{:S(2)}) collective-permute-start(bf16[2,192,384]{2,1,0:T(8,128)(2,1)S(1)} %get-tuple-element.181), channel_id=1, source_target_pairs={{0,8},{1,17},{2,10},{3,19},{4,12},{5,21},{6,14},{7,23},{8,0},{9,25... | collective-permute-start | bytes 884744 | tf_op jit(solution)/shard_map/ppermute | solution.py:887
  117.2 20.6 %collective-permute-start.18 = (bf16[512,768]{1,0:T(8,128)(2,1)S(1)}, bf16[512,768]{1,0:T(8,128)(2,1)S(1)}, u32[]{:S(2)}, u32[]{:S(2)}) collective-permute-start(bf16[512,768]{1,0:T(8,128)(2,1)S(1)} %get-tuple-element.194), channel_id=1, source_target_pairs={{0,1},{1,0},{2,3},{3,2},{4,5},{5,4},{6,7},{7,6},{8,9},{9,8},{10,11... | collective-permute-start | bytes 2359304 | tf_op jit(solution)/shard_map/ppermute | solution.py:911
  125.7 14.8 %collective-permute-start.17 = (bf16[512,768]{1,0:T(8,128)(2,1)S(1)}, bf16[512,768]{1,0:T(8,128)(2,1)S(1)}, u32[]{:S(2)}, u32[]{:S(2)}) collective-permute-start(bf16[512,768]{1,0:T(8,128)(2,1)S(1)} %get-tuple-element.192), channel_id=1, source_target_pairs={{0,1},{1,0},{2,3},{3,2},{4,5},{5,4},{6,7},{7,6},{8,9},{9,8},{10,11... | collective-permute-start | bytes 2359304 | tf_op jit(solution)/shard_map/ppermute | solution.py:911
  125.8 11.1 %collective-permute-start.19 = (bf16[2,48,1152]{2,1,0:T(8,128)(2,1)S(1)}, bf16[2,48,1152]{2,1,0:T(8,128)(2,1)S(1)}, u32[]{:S(2)}, u32[]{:S(2)}) collective-permute-start(bf16[2,48,1152]{2,1,0:T(8,128)(2,1)S(1)} %get-tuple-element.197), channel_id=1, source_target_pairs={{0,8},{1,17},{2,10},{3,19},{4,12},{5,21},{6,14},{7,23},{8,0},{9,25... | collective-permute-start | bytes 663560 | tf_op jit(solution)/shard_map/ppermute | solution.py:887
  127.2 5.1 %collective-permute-start.20 = (bf16[4,48,384]{2,1,0:T(8,128)(2,1)S(1)}, bf16[4,48,384]{2,1,0:T(8,128)(2,1)S(1)}, u32[]{:S(2)}, u32[]{:S(2)}) collective-permute-start(bf16[4,48,384]{2,1,0:T(8,128)(2,1)S(1)} %get-tuple-element.199), channel_id=1, source_target_pairs={{0,4},{1,3},{2,6},{3,1},{4,0},{5,7},{6,2},{7,5},{8,12},{9,11},{10,... | collective-permute-start | bytes 442376 | tf_op jit(solution)/shard_map/ppermute | solution.py:887
  127.6 22.6 %collective-permute-start.22 = (bf16[1,48,1536]{2,1,0:T(8,128)(2,1)S(1)}, bf16[1,48,1536]{2,1,0:T(8,128)(2,1)S(1)}, u32[]{:S(2)}, u32[]{:S(2)}) collective-permute-start(bf16[1,48,1536]{2,1,0:T(8,128)(2,1)S(1)} %get-tuple-element.214), channel_id=1, source_target_pairs={{0,16},{1,9},{2,18},{3,11},{4,20},{5,13},{6,22},{7,15},{8,24},{9,1... | collective-permute-start | bytes 442376 | tf_op jit(solution)/shard_map/ppermute | solution.py:887
  132.4 17.8 %collective-permute-start.23 = (bf16[1,192,384]{2,1,0:T(8,128)(2,1)S(1)}, bf16[1,192,384]{2,1,0:T(8,128)(2,1)S(1)}, u32[]{:S(2)}, u32[]{:S(2)}) collective-permute-start(bf16[1,192,384]{2,1,0:T(8,128)(2,1)S(1)} %get-tuple-element.216), channel_id=1, source_target_pairs={{0,16},{1,9},{2,18},{3,11},{4,20},{5,13},{6,22},{7,15},{8,24},{9,1... | collective-permute-start | bytes 442376 | tf_op jit(solution)/shard_map/ppermute | solution.py:887
  136.9 12.6 %collective-permute-start.24 = (bf16[2,48,384]{2,1,0:T(8,128)(2,1)S(1)}, bf16[2,48,384]{2,1,0:T(8,128)(2,1)S(1)}, u32[]{:S(2)}, u32[]{:S(2)}) collective-permute-start(bf16[2,48,384]{2,1,0:T(8,128)(2,1)S(1)} %get-tuple-element.218), channel_id=1, source_target_pairs={{0,8},{1,17},{2,10},{3,19},{4,12},{5,21},{6,14},{7,23},{8,0},{9,25... | collective-permute-start | bytes 221192 | tf_op jit(solution)/shard_map/ppermute | solution.py:887
  142.8 8.0 %collective-permute-start.21 = (f32[64,384]{1,0:T(8,128)S(1)}, f32[64,384]{1,0:T(8,128)S(1)}, u32[]{:S(2)}, u32[]{:S(2)}) collective-permute-start(f32[64,384]{1,0:T(8,128)S(1)} %get-tuple-element.212.refs_1_), channel_id=1, source_target_pairs={{0,1},{1,0},{2,3},{3,2},{4,5},{5,4},{6,7},{7,6},{8,9},{9,8},{10,11... | collective-permute-start | bytes 294920 | tf_op jit(solution)/shard_map/ppermute | solution.py:911
  142.9 12.4 %collective-permute-start.31 = (bf16[1,48,1152]{2,1,0:T(8,128)(2,1)S(1)}, bf16[1,48,1152]{2,1,0:T(8,128)(2,1)S(1)}, u32[]{:S(2)}, u32[]{:S(2)}) collective-permute-start(bf16[1,48,1152]{2,1,0:T(8,128)(2,1)S(1)} %get-tuple-element.228), channel_id=1, source_target_pairs={{0,16},{1,9},{2,18},{3,11},{4,20},{5,13},{6,22},{7,15},{8,24},{9,1... | collective-permute-start | bytes 331784 | tf_op jit(solution)/shard_map/ppermute | solution.py:887
  150.0 6.7 %collective-permute-start.32 = (bf16[1,48,384]{2,1,0:T(8,128)(2,1)S(1)}, bf16[1,48,384]{2,1,0:T(8,128)(2,1)S(1)}, u32[]{:S(2)}, u32[]{:S(2)}) collective-permute-start(bf16[1,48,384]{2,1,0:T(8,128)(2,1)S(1)} %get-tuple-element.230), channel_id=1, source_target_pairs={{0,16},{1,9},{2,18},{3,11},{4,20},{5,13},{6,22},{7,15},{8,24},{9,1... | collective-permute-start | bytes 110600 | tf_op jit(solution)/shard_map/ppermute | solution.py:887
  150.8 14.8 %collective-permute-start.34 = (bf16[96,1536]{1,0:T(8,128)(2,1)S(1)}, bf16[96,1536]{1,0:T(8,128)(2,1)S(1)}, u32[]{:S(2)}, u32[]{:S(2)}) collective-permute-start(bf16[96,1536]{1,0:T(8,128)(2,1)S(1)} %get-tuple-element.233.refs_1_), channel_id=1, source_target_pairs={{0,1},{1,0},{2,3},{3,2},{4,5},{5,4},{6,7},{7,6},{8,9},{9,8},{10,11... | collective-permute-start | bytes 884744 | tf_op jit(solution)/shard_map/ppermute | solution.py:911
  152.4 5.1 %collective-permute-start.25 = (f32[16,384]{1,0:T(8,128)S(1)}, f32[16,384]{1,0:T(8,128)S(1)}, u32[]{:S(2)}, u32[]{:S(2)}) collective-permute-start(f32[16,384]{1,0:T(8,128)S(1)} %get-tuple-element.224), channel_id=1, source_target_pairs={{0,8},{2,10},{4,12},{6,14},{8,0},{10,2},{12,4},{14,6},{16,24},{18,... | collective-permute-start | bytes 73736 | tf_op jit(solution)/shard_map/ppermute | solution.py:979
  153.7 4.9 %collective-permute-start.26 = (f32[16,384]{1,0:T(8,128)S(1)}, f32[16,384]{1,0:T(8,128)S(1)}, u32[]{:S(2)}, u32[]{:S(2)}) collective-permute-start(f32[16,384]{1,0:T(8,128)S(1)} %get-tuple-element.225), channel_id=1, source_target_pairs={{0,16},{2,18},{4,20},{6,22},{8,24},{10,26},{12,28},{14,30},{16,0},... | collective-permute-start | bytes 73736 | tf_op jit(solution)/shard_map/ppermute | solution.py:979
  155.3 5.6 %collective-permute-start.27 = (f32[16,384]{1,0:T(8,128)S(1)}, f32[16,384]{1,0:T(8,128)S(1)}, u32[]{:S(2)}, u32[]{:S(2)}) collective-permute-start(f32[16,384]{1,0:T(8,128)S(1)} %get-tuple-element.226), channel_id=1, source_target_pairs={{0,24},{2,26},{4,28},{6,30},{8,16},{10,18},{12,20},{14,22},{16,8},... | collective-permute-start | bytes 73736 | tf_op jit(solution)/shard_map/ppermute | solution.py:979
  157.4 9.8 %collective-permute-start.33 = (bf16[48,1536]{1,0:T(8,128)(2,1)S(1)}, bf16[48,1536]{1,0:T(8,128)(2,1)S(1)}, u32[]{:S(2)}, u32[]{:S(2)}) collective-permute-start(bf16[48,1536]{1,0:T(8,128)(2,1)S(1)} %get-tuple-element.232.refs_1_), channel_id=1, source_target_pairs={{0,1},{1,0},{2,3},{3,2},{4,5},{5,4},{6,7},{7,6},{8,9},{9,8},{10,11... | collective-permute-start | bytes 442376 | tf_op jit(solution)/shard_map/ppermute | solution.py:911
  160.9 7.7 %collective-permute-start.28 = (f32[64,384]{1,0:T(8,128)S(1)}, f32[64,384]{1,0:T(8,128)S(1)}, u32[]{:S(2)}, u32[]{:S(2)}) collective-permute-start(f32[64,384]{1,0:T(8,128)S(1)} %constant_dynamic-update-slice_fusion.refs_1_), channel_id=1, source_target_pairs={{0,2},{2,0},{4,6},{6,4},{8,10},{10,8},{12,14},{14,12},{16,18},{18,... | collective-permute-start | bytes 294920 | tf_op jit(solution)/shard_map/ppermute | solution.py:984
  163.3 5.2 %collective-permute-start.29 = (f32[64,384]{1,0:T(8,128)S(1)}, f32[64,384]{1,0:T(8,128)S(1)}, u32[]{:S(2)}, u32[]{:S(2)}) collective-permute-start(f32[64,384]{1,0:T(8,128)S(1)} %constant_dynamic-update-slice_fusion.refs_1_), channel_id=1, source_target_pairs={{0,4},{2,6},{4,0},{6,2},{8,12},{10,14},{12,8},{14,10},{16,20},{18,... | collective-permute-start | bytes 294920 | tf_op jit(solution)/shard_map/ppermute | solution.py:984
  164.1 5.5 %collective-permute-start.30 = (f32[64,384]{1,0:T(8,128)S(1)}, f32[64,384]{1,0:T(8,128)S(1)}, u32[]{:S(2)}, u32[]{:S(2)}) collective-permute-start(f32[64,384]{1,0:T(8,128)S(1)} %constant_dynamic-update-slice_fusion.refs_1_), channel_id=1, source_target_pairs={{0,6},{2,4},{4,2},{6,0},{8,14},{10,12},{12,10},{14,8},{16,22},{18,... | collective-permute-start | bytes 294920 | tf_op jit(solution)/shard_map/ppermute | solution.py:984
  (14 other events, 142.6 us)
